TPU v7x, 768 devices: a whole 4x8x12 slice. The times are simulated.
768 devices in a mesh: box: 192 (over y, z, core), grp: 4 (over x).
Axes of the slice: x: 4, y: 8, z: 12, core: 2. Of those that a mesh axis runs over, the one named last changes fastest.
Arguments:
- conserved_state: float32 [5, 1536, 32, 128], P(None, 'box', 'grp'), may hold values from -17 to 95, as said below
- box_source: int32 [384], replicated, may hold values from 0 to 383, as said below
Outputs:
- regridded: float32 [5, 1536, 32, 128], P(None, 'box', 'grp')
- potential: float32 [1536, 32, 128], P('box', 'grp')
Inputs may be any that keep to these rules, and one draw needn't show every extreme that they name: `conserved_state`: the pressure of every cell is positive and so is its density. `box_source`: A permutation of the boxes. The box at position k comes from owner k // 2 or an owner next to it (no wrap); across each boundary between owners at most 1 boxes move in each direction, and exactly 1 in both directions across some boundary.
All inputs are finite; a program needn't handle non-finite values.
Results may differ from a plain program's by a relative error of at most 0.0003.
Values sent between devices are 32-bit elements; how exact they have to be, the bound alone decides.
No kernel may reach another device: no remote copies, remote signals or barrier semaphores. Data moves between devices by JAX's collectives and lax.ppermute only.
A program may use at most 32 MiB of HBM per device.

v0:
```python
import jax
import jax.numpy as jnp
from jax import lax
from jax.sharding import PartitionSpec as P

COARSE = 4
POST = 2


GAMMA = 5.0 / 3.0
COURANT = 0.3
OMEGA = 2.0 / 3.0
FOUR_PI_G = 2.0


def with_halo(value, sides, width, wrap):
    for axis, dim in sides:
        count, length = (lax.axis_size(axis), value.shape[dim])
        up = [(i, (i + 1) % count) for i in range(count if wrap else count - 1)]
        down = [(j, i) for i, j in up]
        last = lax.slice_in_dim(value, length - width, length, axis=dim)
        first = lax.slice_in_dim(value, 0, width, axis=dim)
        before = lax.ppermute(last, axis, up)
        after = lax.ppermute(first, axis, down)
        value = jnp.concatenate([before, value, after], axis=dim)
    return value


def minmod(left_diff, right_diff):
    return (
        0.5
        * (jnp.sign(left_diff) + jnp.sign(right_diff))
        * jnp.minimum(jnp.abs(left_diff), jnp.abs(right_diff))
    )


def primitive(conserved):
    density = conserved[0]
    velocity = conserved[1:4] / density
    kinetic = 0.5 * jnp.sum(conserved[1:4] * velocity, axis=0)
    pressure = (GAMMA - 1.0) * (conserved[4] - kinetic)
    return jnp.concatenate([density[None], velocity, pressure[None]], axis=0)


def signal_speed(conserved):
    prim_state = primitive(conserved)
    sound_speed = jnp.sqrt(GAMMA * prim_state[4] / prim_state[0])
    return jnp.max(jnp.abs(prim_state[1:4]), axis=0) + sound_speed


def side_terms(face_state, normal):
    density = face_state[0]
    velocity = face_state[1:4]
    pressure = face_state[4]
    normal_speed = velocity[normal]
    energy = pressure / (GAMMA - 1.0) + 0.5 * density * jnp.sum(velocity * velocity, axis=0)
    conserved = jnp.concatenate([density[None], density[None] * velocity, energy[None]], axis=0)
    momentum_flux = [
        density * normal_speed * velocity[component]
        + pressure * (1.0 if component == normal else 0.0)
        for component in range(3)
    ]
    flux_terms = jnp.stack(
        [density * normal_speed] + momentum_flux + [normal_speed * (energy + pressure)], axis=0
    )
    sound_speed = jnp.sqrt(GAMMA * pressure / density)
    return (conserved, flux_terms, normal_speed, sound_speed)


def hll_flux(left_state, right_state, normal):
    cons_left, flux_left, speed_left, sound_left = side_terms(left_state, normal)
    cons_right, flux_right, speed_right, sound_right = side_terms(right_state, normal)
    lowest = jnp.minimum(jnp.minimum(speed_left - sound_left, speed_right - sound_right), 0.0)
    highest = jnp.maximum(jnp.maximum(speed_left + sound_left, speed_right + sound_right), 0.0)
    return (
        highest * flux_left - lowest * flux_right + highest * lowest * (cons_right - cons_left)
    ) / (highest - lowest)


def flux_balance(slab_cells, normal):
    axis_number = normal + 1
    length = slab_cells.shape[axis_number] - 4
    prim_state = primitive(slab_cells)
    differences = lax.slice_in_dim(prim_state, 1, length + 4, axis=axis_number) - lax.slice_in_dim(
        prim_state, 0, length + 3, axis=axis_number
    )
    slopes = minmod(
        lax.slice_in_dim(differences, 0, length + 2, axis=axis_number),
        lax.slice_in_dim(differences, 1, length + 3, axis=axis_number),
    )
    left_state = lax.slice_in_dim(
        prim_state, 1, length + 2, axis=axis_number
    ) + 0.5 * lax.slice_in_dim(slopes, 0, length + 1, axis=axis_number)
    right_state = lax.slice_in_dim(
        prim_state, 2, length + 3, axis=axis_number
    ) - 0.5 * lax.slice_in_dim(slopes, 1, length + 2, axis=axis_number)
    fluxes = hll_flux(left_state, right_state, normal)
    return lax.slice_in_dim(fluxes, 1, length + 1, axis=axis_number) - lax.slice_in_dim(
        fluxes, 0, length, axis=axis_number
    )


def advance(padded, time_step):
    fields = padded[:5]
    potential = padded[5]
    interior = fields[:, 2:-2, 2:-2, 2:-2]
    balance = flux_balance(fields[:, :, 2:-2, 2:-2], 0)
    balance = balance + flux_balance(fields[:, 2:-2, :, 2:-2], 1)
    balance = balance + flux_balance(fields[:, 2:-2, 2:-2, :], 2)
    pull_first = 0.5 * (potential[1:-3, 2:-2, 2:-2] - potential[3:-1, 2:-2, 2:-2])
    pull_second = 0.5 * (potential[2:-2, 1:-3, 2:-2] - potential[2:-2, 3:-1, 2:-2])
    pull_third = 0.5 * (potential[2:-2, 2:-2, 1:-3] - potential[2:-2, 2:-2, 3:-1])
    gravity = jnp.stack([pull_first, pull_second, pull_third], axis=0)
    gained = jnp.concatenate(
        [
            jnp.zeros_like(interior[:1]),
            interior[0][None] * gravity,
            jnp.sum(interior[1:4] * gravity, axis=0)[None],
        ],
        axis=0,
    )
    return interior - time_step * balance + time_step * gained


def operator(padded):
    center = padded[1:-1, 1:-1, 1:-1]
    beside = padded[2:, 1:-1, 1:-1] + padded[:-2, 1:-1, 1:-1]
    beside = beside + padded[1:-1, 2:, 1:-1] + padded[1:-1, :-2, 1:-1]
    beside = beside + padded[1:-1, 1:-1, 2:] + padded[1:-1, 1:-1, :-2]
    return 6.0 * center - beside


def wrap_third(rimmed):
    return jnp.concatenate([rimmed[:, :, -1:], rimmed, rimmed[:, :, :1]], axis=2)


def restrict(grid_field):
    size_x, size_y, size_z = grid_field.shape
    grouped = grid_field.reshape(size_x // 2, 2, size_y // 2, 2, size_z // 2, 2)
    return 0.5 * jnp.sum(grouped, axis=(1, 3, 5))


def prolong(grid_field):
    return jnp.repeat(jnp.repeat(jnp.repeat(grid_field, 2, axis=0), 2, axis=1), 2, axis=2)


def fine_operator(grid_field):
    rimmed = with_halo(grid_field, (("box", 0), ("grp", 1)), 1, True)
    return operator(wrap_third(rimmed))


def fine_sweep(grid_field, source):
    return grid_field + OMEGA / 6.0 * (source - fine_operator(grid_field))


def spread_sweep(grid_field, source):
    rimmed = with_halo(grid_field, (("box", 0), ("grp", 1)), 1, True)
    return grid_field + OMEGA / 6.0 * (source - operator(wrap_third(rimmed)))


def shards(conserved_state, box_source):
    density = conserved_state[0]
    cell_count = density.size * lax.axis_size("box") * lax.axis_size("grp")
    total_mass = lax.psum(jnp.sum(density), ("box", "grp"))
    mean_density = total_mass / cell_count
    source = FOUR_PI_G * (mean_density - density)
    top_speed = lax.pmax(jnp.max(signal_speed(conserved_state)), ("box", "grp"))
    time_step = COURANT / top_speed
    potential = OMEGA / 6.0 * source
    potential = fine_sweep(potential, source)
    residue = source - fine_operator(potential)
    coarse_source = restrict(residue)
    correction = OMEGA / 6.0 * coarse_source
    for number in range(COARSE - 1):
        correction = spread_sweep(correction, coarse_source)
    potential = potential + prolong(correction)
    for number in range(POST):
        potential = fine_sweep(potential, source)
    stacked = jnp.concatenate([conserved_state, potential[None]], axis=0)
    rimmed = with_halo(stacked, (("box", 1), ("grp", 2)), 2, True)
    rimmed = jnp.concatenate([rimmed[..., -2:], rimmed, rimmed[..., :2]], axis=3)
    updated = advance(rimmed, time_step)
    box_count = lax.axis_size("box")
    slot_count = box_source.shape[0] // box_count
    box_rows = updated.shape[1] // slot_count
    box_data = updated.reshape(5, slot_count, box_rows, updated.shape[2], updated.shape[3])
    own_index = lax.axis_index("box")
    own_sources = lax.dynamic_slice_in_dim(box_source, own_index * slot_count, slot_count)
    candidates = with_halo(box_data, (("box", 1),), slot_count, False)
    pick_index = own_sources - (own_index - 1) * slot_count
    picked = jnp.take(candidates, pick_index, axis=1)
    regridded = picked.reshape(5, slot_count * box_rows, updated.shape[2], updated.shape[3])
    return (regridded, potential)


def solution(mesh):
    in_specs = (P(None, "box", "grp", None), P())
    out_specs = (P(None, "box", "grp", None), P("box", "grp", None))
    return jax.shard_map(shards, mesh=mesh, in_specs=in_specs, out_specs=out_specs, check_vma=False)
```

profile of v0, /device:TPU:32, one launch (start us, length us, event | category | flops | bytes accessed | tf_op | source)
XLA Modules:
  0.0 412.7 jit_solution(9309384538823993085)
XLA Ops:
  0.6 1.4 slice_bitcast_fusion.1
  2.1 117.6 %psum.7 = f32[]{:T(128)} all-reduce(f32[]{:T(128)} %get-tuple-element.107), channel_id=1, replica_groups=mesh['box'=192,'grp'=4] {'box','grp'}, use_global_device_ids=true, to_apply=%region_5.0 | all-reduce | flops 1 | bytes 8 | tf_op jit(solution)/shard_map/psum | solution.py:164
  121.1 1.9 collective-permute-start.1
  123.0 7.0 %collective-permute-start = (f32[1,8,128]{2,1,0:T(8,128)S(1)}, f32[1,8,128]{2,1,0:T(8,128)S(1)}, u32[]{:S(2)}, u32[]{:S(2)}) collective-permute-start(f32[1,8,128]{2,1,0:T(8,128)S(1)} %get-tuple-element.132), channel_id=1, source_target_pairs={{4,0},{8,4},{12,8},{16,12},{20,16},{24,20},{28,24},{32,28},{36,32}... | collective-permute-start | bytes 12296 | tf_op jit(solution)/shard_map/ppermute | solution.py:24
  131.3 2.7 collective-permute-start.3
  134.0 4.3 %collective-permute-start.2 = (f32[10,1,128]{2,1,0:T(1,128)S(1)}, f32[10,1,128]{2,1,0:T(1,128)S(1)}, u32[]{:S(2)}, u32[]{:S(2)}) collective-permute-start(f32[10,1,128]{2,1,0:T(1,128)S(1)} %get-tuple-element.124), channel_id=1, source_target_pairs={{1,0},{2,1},{3,2},{0,3},{5,4},{6,5},{7,6},{4,7},{9,8},{10,9},{11,1... | collective-permute-start | bytes 15368 | tf_op jit(solution)/shard_map/ppermute | solution.py:24
  138.4 1.3 collective-permute-done.2
  140.7 1.9 collective-permute-start.5
  142.6 7.0 %collective-permute-start.4 = (f32[1,8,128]{2,1,0:T(8,128)S(1)}, f32[1,8,128]{2,1,0:T(8,128)S(1)}, u32[]{:S(2)}, u32[]{:S(2)}) collective-permute-start(f32[1,8,128]{2,1,0:T(8,128)S(1)} %get-tuple-element.130), channel_id=1, source_target_pairs={{4,0},{8,4},{12,8},{16,12},{20,16},{24,20},{28,24},{32,28},{36,32}... | collective-permute-start | bytes 12296 | tf_op jit(solution)/shard_map/ppermute | solution.py:24
  150.9 1.9 collective-permute-start.7
  152.8 5.4 %collective-permute-start.6 = (f32[10,1,128]{2,1,0:T(1,128)S(1)}, f32[10,1,128]{2,1,0:T(1,128)S(1)}, u32[]{:S(2)}, u32[]{:S(2)}) collective-permute-start(f32[10,1,128]{2,1,0:T(1,128)S(1)} %get-tuple-element.122), channel_id=1, source_target_pairs={{1,0},{2,1},{3,2},{0,3},{5,4},{6,5},{7,6},{4,7},{9,8},{10,9},{11,1... | collective-permute-start | bytes 15368 | tf_op jit(solution)/shard_map/ppermute | solution.py:24
  158.2 1.3 collective-permute-done.6
  159.8 2.1 reshape.66
  162.1 1.9 collective-permute-start.9
  164.1 7.0 %collective-permute-start.8 = (f32[1,4,64]{2,1,0:T(4,128)S(1)}, f32[1,4,64]{2,1,0:T(4,128)S(1)}, u32[]{:S(2)}, u32[]{:S(2)}) collective-permute-start(f32[1,4,64]{2,1,0:T(4,128)S(1)} %get-tuple-element.150), channel_id=1, source_target_pairs={{4,0},{8,4},{12,8},{16,12},{20,16},{24,20},{28,24},{32,28},{36,32}... | collective-permute-start | bytes 3080 | tf_op jit(solution)/shard_map/ppermute | solution.py:24
  172.3 3.6 collective-permute-start.11
  175.9 3.7 collective-permute-start.10
  179.7 1.7 collective-permute-done.10
  181.6 1.9 collective-permute-start.13
  183.5 7.0 %collective-permute-start.12 = (f32[1,4,64]{2,1,0:T(4,128)S(1)}, f32[1,4,64]{2,1,0:T(4,128)S(1)}, u32[]{:S(2)}, u32[]{:S(2)}) collective-permute-start(f32[1,4,64]{2,1,0:T(4,128)S(1)} %get-tuple-element.148), channel_id=1, source_target_pairs={{4,0},{8,4},{12,8},{16,12},{20,16},{24,20},{28,24},{32,28},{36,32}... | collective-permute-start | bytes 3080 | tf_op jit(solution)/shard_map/ppermute | solution.py:24
  191.8 3.9 collective-permute-start.15
  195.7 3.1 collective-permute-start.14
  198.9 2.3 collective-permute-done.14
  201.5 1.9 collective-permute-start.17
  203.4 7.0 %collective-permute-start.16 = (f32[1,4,64]{2,1,0:T(4,128)S(1)}, f32[1,4,64]{2,1,0:T(4,128)S(1)}, u32[]{:S(2)}, u32[]{:S(2)}) collective-permute-start(f32[1,4,64]{2,1,0:T(4,128)S(1)} %get-tuple-element.146), channel_id=1, source_target_pairs={{4,0},{8,4},{12,8},{16,12},{20,16},{24,20},{28,24},{32,28},{36,32}... | collective-permute-start | bytes 3080 | tf_op jit(solution)/shard_map/ppermute | solution.py:24
  211.7 3.1 collective-permute-start.19
  214.8 3.9 collective-permute-start.18
  218.7 1.5 collective-permute-done.18
  220.9 1.9 collective-permute-start.21
  222.9 7.0 %collective-permute-start.20 = (f32[1,8,128]{2,1,0:T(8,128)S(1)}, f32[1,8,128]{2,1,0:T(8,128)S(1)}, u32[]{:S(2)}, u32[]{:S(2)}) collective-permute-start(f32[1,8,128]{2,1,0:T(8,128)S(1)} %get-tuple-element.128), channel_id=1, source_target_pairs={{4,0},{8,4},{12,8},{16,12},{20,16},{24,20},{28,24},{32,28},{36,32}... | collective-permute-start | bytes 12296 | tf_op jit(solution)/shard_map/ppermute | solution.py:24
  231.2 3.1 collective-permute-start.23
  234.3 3.9 collective-permute-start.22
  238.2 1.6 collective-permute-done.22
  240.0 1.9 collective-permute-start.25
  242.0 7.0 %collective-permute-start.24 = (f32[1,8,128]{2,1,0:T(8,128)S(1)}, f32[1,8,128]{2,1,0:T(8,128)S(1)}, u32[]{:S(2)}, u32[]{:S(2)}) collective-permute-start(f32[1,8,128]{2,1,0:T(8,128)S(1)} %get-tuple-element.126), channel_id=1, source_target_pairs={{4,0},{8,4},{12,8},{16,12},{20,16},{24,20},{28,24},{32,28},{36,32}... | collective-permute-start | bytes 12296 | tf_op jit(solution)/shard_map/ppermute | solution.py:24
  250.3 3.3 collective-permute-start.27
  253.6 3.7 collective-permute-start.26
  257.3 1.8 collective-permute-done.26
  259.4 1.9 collective-permute-start.28
  261.3 7.0 %collective-permute-start.29 = (f32[6,2,8,128]{3,2,1,0:T(8,128)S(1)}, f32[6,2,8,128]{3,2,1,0:T(8,128)S(1)}, u32[]{:S(2)}, u32[]{:S(2)}) collective-permute-start(f32[6,2,8,128]{3,2,1,0:T(8,128)S(1)} %get-tuple-element.83), channel_id=1, source_target_pairs={{4,0},{8,4},{12,8},{16,12},{20,16},{24,20},{28,24},{32,28},{36,32}... | collective-permute-start | bytes 147464 | tf_op jit(solution)/shard_map/ppermute | solution.py:24
  268.3 1.7 collective-permute-done.29
  270.0 3.9 collective-permute-start.30
  274.0 3.1 collective-permute-start.31
  277.7 2.5 collective-permute-done.31
  284.1 109.0 %pmax.7 = f32[]{:T(128)} all-reduce(f32[]{:T(128)} %fusion.87), channel_id=1, replica_groups=mesh['box'=192,'grp'=4] {'box','grp'}, use_global_device_ids=true, to_apply=%region_3.0 | all-reduce | flops 1 | bytes 8 | tf_op jit(solution)/shard_map/pmax | solution.py:167
  399.4 1.9 collective-permute-start.33
  401.4 2.4 collective-permute-start.32
  404.7 6.6 %collective-permute-done.32 = f32[5,2,4,8,128]{4,3,2,1,0:T(8,128)S(1)} collective-permute-done((f32[5,2,4,8,128]{4,3,2,1,0:T(8,128)S(1)}, f32[5,2,4,8,128]{4,3,2,1,0:T(8,128)S(1)}, u32[]{:S(2)}, u32[]{:S(2)}) %collective-permute-start.32) | collective-permute-done | bytes 163872 | tf_op jit(solution)/shard_map/ppermute | solution.py:23
  (168 shorter events, 24.8 us)
Async XLA Ops:
  0.6 159.0 %copy-start = (f32[5,8,8,128]{3,2,1,0:T(8,128)S(1)}, f32[5,8,8,128]{3,2,1,0:T(8,128)}, u32[]{:S(2)}) copy-start(f32[5,8,8,128]{3,2,1,0:T(8,128)} %param.2) | copy-start | bytes 491524
  121.1 8.9 %collective-permute-start.1 = (f32[1,8,128]{2,1,0:T(8,128)S(1)}, f32[1,8,128]{2,1,0:T(8,128)S(1)}, u32[]{:S(2)}, u32[]{:S(2)}) collective-permute-start(f32[1,8,128]{2,1,0:T(8,128)S(1)} %get-tuple-element.131), channel_id=1, source_target_pairs={{0,4},{4,8},{8,12},{12,16},{16,20},{20,24},{24,28},{28,32},{32,36}... | collective-permute-start | bytes 12296 | tf_op jit(solution)/shard_map/ppermute | solution.py:23
  123.0 8.3 %collective-permute-start = (f32[1,8,128]{2,1,0:T(8,128)S(1)}, f32[1,8,128]{2,1,0:T(8,128)S(1)}, u32[]{:S(2)}, u32[]{:S(2)}) collective-permute-start(f32[1,8,128]{2,1,0:T(8,128)S(1)} %get-tuple-element.132), channel_id=1, source_target_pairs={{4,0},{8,4},{12,8},{16,12},{20,16},{24,20},{28,24},{32,28},{36,32}... | collective-permute-start | bytes 12296 | tf_op jit(solution)/shard_map/ppermute | solution.py:24
  131.3 7.1 %collective-permute-start.3 = (f32[10,1,128]{2,1,0:T(1,128)S(1)}, f32[10,1,128]{2,1,0:T(1,128)S(1)}, u32[]{:S(2)}, u32[]{:S(2)}) collective-permute-start(f32[10,1,128]{2,1,0:T(1,128)S(1)} %get-tuple-element.123), channel_id=1, source_target_pairs={{0,1},{1,2},{2,3},{3,0},{4,5},{5,6},{6,7},{7,4},{8,9},{9,10},{10,1... | collective-permute-start | bytes 15368 | tf_op jit(solution)/shard_map/ppermute | solution.py:23
  134.0 5.6 %collective-permute-start.2 = (f32[10,1,128]{2,1,0:T(1,128)S(1)}, f32[10,1,128]{2,1,0:T(1,128)S(1)}, u32[]{:S(2)}, u32[]{:S(2)}) collective-permute-start(f32[10,1,128]{2,1,0:T(1,128)S(1)} %get-tuple-element.124), channel_id=1, source_target_pairs={{1,0},{2,1},{3,2},{0,3},{5,4},{6,5},{7,6},{4,7},{9,8},{10,9},{11,1... | collective-permute-start | bytes 15368 | tf_op jit(solution)/shard_map/ppermute | solution.py:24
  140.7 8.9 %collective-permute-start.5 = (f32[1,8,128]{2,1,0:T(8,128)S(1)}, f32[1,8,128]{2,1,0:T(8,128)S(1)}, u32[]{:S(2)}, u32[]{:S(2)}) collective-permute-start(f32[1,8,128]{2,1,0:T(8,128)S(1)} %get-tuple-element.129), channel_id=1, source_target_pairs={{0,4},{4,8},{8,12},{12,16},{16,20},{20,24},{24,28},{28,32},{32,36}... | collective-permute-start | bytes 12296 | tf_op jit(solution)/shard_map/ppermute | solution.py:23
  142.6 8.3 %collective-permute-start.4 = (f32[1,8,128]{2,1,0:T(8,128)S(1)}, f32[1,8,128]{2,1,0:T(8,128)S(1)}, u32[]{:S(2)}, u32[]{:S(2)}) collective-permute-start(f32[1,8,128]{2,1,0:T(8,128)S(1)} %get-tuple-element.130), channel_id=1, source_target_pairs={{4,0},{8,4},{12,8},{16,12},{20,16},{24,20},{28,24},{32,28},{36,32}... | collective-permute-start | bytes 12296 | tf_op jit(solution)/shard_map/ppermute | solution.py:24
  150.9 7.3 %collective-permute-start.7 = (f32[10,1,128]{2,1,0:T(1,128)S(1)}, f32[10,1,128]{2,1,0:T(1,128)S(1)}, u32[]{:S(2)}, u32[]{:S(2)}) collective-permute-start(f32[10,1,128]{2,1,0:T(1,128)S(1)} %get-tuple-element.121), channel_id=1, source_target_pairs={{0,1},{1,2},{2,3},{3,0},{4,5},{5,6},{6,7},{7,4},{8,9},{9,10},{10,1... | collective-permute-start | bytes 15368 | tf_op jit(solution)/shard_map/ppermute | solution.py:23
  152.8 6.7 %collective-permute-start.6 = (f32[10,1,128]{2,1,0:T(1,128)S(1)}, f32[10,1,128]{2,1,0:T(1,128)S(1)}, u32[]{:S(2)}, u32[]{:S(2)}) collective-permute-start(f32[10,1,128]{2,1,0:T(1,128)S(1)} %get-tuple-element.122), channel_id=1, source_target_pairs={{1,0},{2,1},{3,2},{0,3},{5,4},{6,5},{7,6},{4,7},{9,8},{10,9},{11,1... | collective-permute-start | bytes 15368 | tf_op jit(solution)/shard_map/ppermute | solution.py:24
  162.1 8.9 %collective-permute-start.9 = (f32[1,4,64]{2,1,0:T(4,128)S(1)}, f32[1,4,64]{2,1,0:T(4,128)S(1)}, u32[]{:S(2)}, u32[]{:S(2)}) collective-permute-start(f32[1,4,64]{2,1,0:T(4,128)S(1)} %get-tuple-element.149), channel_id=1, source_target_pairs={{0,4},{4,8},{8,12},{12,16},{16,20},{20,24},{24,28},{28,32},{32,36}... | collective-permute-start | bytes 3080 | tf_op jit(solution)/shard_map/ppermute | solution.py:23
  164.1 8.3 %collective-permute-start.8 = (f32[1,4,64]{2,1,0:T(4,128)S(1)}, f32[1,4,64]{2,1,0:T(4,128)S(1)}, u32[]{:S(2)}, u32[]{:S(2)}) collective-permute-start(f32[1,4,64]{2,1,0:T(4,128)S(1)} %get-tuple-element.150), channel_id=1, source_target_pairs={{4,0},{8,4},{12,8},{16,12},{20,16},{24,20},{28,24},{32,28},{36,32}... | collective-permute-start | bytes 3080 | tf_op jit(solution)/shard_map/ppermute | solution.py:24
  172.3 7.3 %collective-permute-start.11 = (f32[6,1,64]{2,1,0:T(1,128)S(1)}, f32[6,1,64]{2,1,0:T(1,128)S(1)}, u32[]{:S(2)}, u32[]{:S(2)}) collective-permute-start(f32[6,1,64]{2,1,0:T(1,128)S(1)} %get-tuple-element.143), channel_id=1, source_target_pairs={{0,1},{1,2},{2,3},{3,0},{4,5},{5,6},{6,7},{7,4},{8,9},{9,10},{10,1... | collective-permute-start | bytes 4616 | tf_op jit(solution)/shard_map/ppermute | solution.py:23
  175.9 5.5 %collective-permute-start.10 = (f32[6,1,64]{2,1,0:T(1,128)S(1)}, f32[6,1,64]{2,1,0:T(1,128)S(1)}, u32[]{:S(2)}, u32[]{:S(2)}) collective-permute-start(f32[6,1,64]{2,1,0:T(1,128)S(1)} %get-tuple-element.144), channel_id=1, source_target_pairs={{1,0},{2,1},{3,2},{0,3},{5,4},{6,5},{7,6},{4,7},{9,8},{10,9},{11,1... | collective-permute-start | bytes 4616 | tf_op jit(solution)/shard_map/ppermute | solution.py:24
  181.6 8.9 %collective-permute-start.13 = (f32[1,4,64]{2,1,0:T(4,128)S(1)}, f32[1,4,64]{2,1,0:T(4,128)S(1)}, u32[]{:S(2)}, u32[]{:S(2)}) collective-permute-start(f32[1,4,64]{2,1,0:T(4,128)S(1)} %get-tuple-element.147), channel_id=1, source_target_pairs={{0,4},{4,8},{8,12},{12,16},{16,20},{20,24},{24,28},{28,32},{32,36}... | collective-permute-start | bytes 3080 | tf_op jit(solution)/shard_map/ppermute | solution.py:23
  183.5 8.3 %collective-permute-start.12 = (f32[1,4,64]{2,1,0:T(4,128)S(1)}, f32[1,4,64]{2,1,0:T(4,128)S(1)}, u32[]{:S(2)}, u32[]{:S(2)}) collective-permute-start(f32[1,4,64]{2,1,0:T(4,128)S(1)} %get-tuple-element.148), channel_id=1, source_target_pairs={{4,0},{8,4},{12,8},{16,12},{20,16},{24,20},{28,24},{32,28},{36,32}... | collective-permute-start | bytes 3080 | tf_op jit(solution)/shard_map/ppermute | solution.py:24
  191.8 7.1 %collective-permute-start.15 = (f32[6,1,64]{2,1,0:T(1,128)S(1)}, f32[6,1,64]{2,1,0:T(1,128)S(1)}, u32[]{:S(2)}, u32[]{:S(2)}) collective-permute-start(f32[6,1,64]{2,1,0:T(1,128)S(1)} %get-tuple-element.141), channel_id=1, source_target_pairs={{0,1},{1,2},{2,3},{3,0},{4,5},{5,6},{6,7},{7,4},{8,9},{9,10},{10,1... | collective-permute-start | bytes 4616 | tf_op jit(solution)/shard_map/ppermute | solution.py:23
  195.7 5.5 %collective-permute-start.14 = (f32[6,1,64]{2,1,0:T(1,128)S(1)}, f32[6,1,64]{2,1,0:T(1,128)S(1)}, u32[]{:S(2)}, u32[]{:S(2)}) collective-permute-start(f32[6,1,64]{2,1,0:T(1,128)S(1)} %get-tuple-element.142), channel_id=1, source_target_pairs={{1,0},{2,1},{3,2},{0,3},{5,4},{6,5},{7,6},{4,7},{9,8},{10,9},{11,1... | collective-permute-start | bytes 4616 | tf_op jit(solution)/shard_map/ppermute | solution.py:24
  201.5 8.9 %collective-permute-start.17 = (f32[1,4,64]{2,1,0:T(4,128)S(1)}, f32[1,4,64]{2,1,0:T(4,128)S(1)}, u32[]{:S(2)}, u32[]{:S(2)}) collective-permute-start(f32[1,4,64]{2,1,0:T(4,128)S(1)} %get-tuple-element.145), channel_id=1, source_target_pairs={{0,4},{4,8},{8,12},{12,16},{16,20},{20,24},{24,28},{28,32},{32,36}... | collective-permute-start | bytes 3080 | tf_op jit(solution)/shard_map/ppermute | solution.py:23
  203.4 8.3 %collective-permute-start.16 = (f32[1,4,64]{2,1,0:T(4,128)S(1)}, f32[1,4,64]{2,1,0:T(4,128)S(1)}, u32[]{:S(2)}, u32[]{:S(2)}) collective-permute-start(f32[1,4,64]{2,1,0:T(4,128)S(1)} %get-tuple-element.146), channel_id=1, source_target_pairs={{4,0},{8,4},{12,8},{16,12},{20,16},{24,20},{28,24},{32,28},{36,32}... | collective-permute-start | bytes 3080 | tf_op jit(solution)/shard_map/ppermute | solution.py:24
  211.7 7.1 %collective-permute-start.19 = (f32[6,1,64]{2,1,0:T(1,128)S(1)}, f32[6,1,64]{2,1,0:T(1,128)S(1)}, u32[]{:S(2)}, u32[]{:S(2)}) collective-permute-start(f32[6,1,64]{2,1,0:T(1,128)S(1)} %get-tuple-element.139), channel_id=1, source_target_pairs={{0,1},{1,2},{2,3},{3,0},{4,5},{5,6},{6,7},{7,4},{8,9},{9,10},{10,1... | collective-permute-start | bytes 4616 | tf_op jit(solution)/shard_map/ppermute | solution.py:23
  214.8 5.5 %collective-permute-start.18 = (f32[6,1,64]{2,1,0:T(1,128)S(1)}, f32[6,1,64]{2,1,0:T(1,128)S(1)}, u32[]{:S(2)}, u32[]{:S(2)}) collective-permute-start(f32[6,1,64]{2,1,0:T(1,128)S(1)} %get-tuple-element.140), channel_id=1, source_target_pairs={{1,0},{2,1},{3,2},{0,3},{5,4},{6,5},{7,6},{4,7},{9,8},{10,9},{11,1... | collective-permute-start | bytes 4616 | tf_op jit(solution)/shard_map/ppermute | solution.py:24
  220.9 8.9 %collective-permute-start.21 = (f32[1,8,128]{2,1,0:T(8,128)S(1)}, f32[1,8,128]{2,1,0:T(8,128)S(1)}, u32[]{:S(2)}, u32[]{:S(2)}) collective-permute-start(f32[1,8,128]{2,1,0:T(8,128)S(1)} %get-tuple-element.127), channel_id=1, source_target_pairs={{0,4},{4,8},{8,12},{12,16},{16,20},{20,24},{24,28},{28,32},{32,36}... | collective-permute-start | bytes 12296 | tf_op jit(solution)/shard_map/ppermute | solution.py:23
  222.9 8.3 %collective-permute-start.20 = (f32[1,8,128]{2,1,0:T(8,128)S(1)}, f32[1,8,128]{2,1,0:T(8,128)S(1)}, u32[]{:S(2)}, u32[]{:S(2)}) collective-permute-start(f32[1,8,128]{2,1,0:T(8,128)S(1)} %get-tuple-element.128), channel_id=1, source_target_pairs={{4,0},{8,4},{12,8},{16,12},{20,16},{24,20},{28,24},{32,28},{36,32}... | collective-permute-start | bytes 12296 | tf_op jit(solution)/shard_map/ppermute | solution.py:24
  231.2 7.1 %collective-permute-start.23 = (f32[10,1,128]{2,1,0:T(1,128)S(1)}, f32[10,1,128]{2,1,0:T(1,128)S(1)}, u32[]{:S(2)}, u32[]{:S(2)}) collective-permute-start(f32[10,1,128]{2,1,0:T(1,128)S(1)} %get-tuple-element.119), channel_id=1, source_target_pairs={{0,1},{1,2},{2,3},{3,0},{4,5},{5,6},{6,7},{7,4},{8,9},{9,10},{10,1... | collective-permute-start | bytes 15368 | tf_op jit(solution)/shard_map/ppermute | solution.py:23
  234.3 5.5 %collective-permute-start.22 = (f32[10,1,128]{2,1,0:T(1,128)S(1)}, f32[10,1,128]{2,1,0:T(1,128)S(1)}, u32[]{:S(2)}, u32[]{:S(2)}) collective-permute-start(f32[10,1,128]{2,1,0:T(1,128)S(1)} %get-tuple-element.120), channel_id=1, source_target_pairs={{1,0},{2,1},{3,2},{0,3},{5,4},{6,5},{7,6},{4,7},{9,8},{10,9},{11,1... | collective-permute-start | bytes 15368 | tf_op jit(solution)/shard_map/ppermute | solution.py:24
  240.0 8.9 %collective-permute-start.25 = (f32[1,8,128]{2,1,0:T(8,128)S(1)}, f32[1,8,128]{2,1,0:T(8,128)S(1)}, u32[]{:S(2)}, u32[]{:S(2)}) collective-permute-start(f32[1,8,128]{2,1,0:T(8,128)S(1)} %get-tuple-element.125), channel_id=1, source_target_pairs={{0,4},{4,8},{8,12},{12,16},{16,20},{20,24},{24,28},{28,32},{32,36}... | collective-permute-start | bytes 12296 | tf_op jit(solution)/shard_map/ppermute | solution.py:23
  242.0 8.3 %collective-permute-start.24 = (f32[1,8,128]{2,1,0:T(8,128)S(1)}, f32[1,8,128]{2,1,0:T(8,128)S(1)}, u32[]{:S(2)}, u32[]{:S(2)}) collective-permute-start(f32[1,8,128]{2,1,0:T(8,128)S(1)} %get-tuple-element.126), channel_id=1, source_target_pairs={{4,0},{8,4},{12,8},{16,12},{20,16},{24,20},{28,24},{32,28},{36,32}... | collective-permute-start | bytes 12296 | tf_op jit(solution)/shard_map/ppermute | solution.py:24
  250.3 7.1 %collective-permute-start.27 = (f32[10,1,128]{2,1,0:T(1,128)S(1)}, f32[10,1,128]{2,1,0:T(1,128)S(1)}, u32[]{:S(2)}, u32[]{:S(2)}) collective-permute-start(f32[10,1,128]{2,1,0:T(1,128)S(1)} %get-tuple-element.117), channel_id=1, source_target_pairs={{0,1},{1,2},{2,3},{3,0},{4,5},{5,6},{6,7},{7,4},{8,9},{9,10},{10,1... | collective-permute-start | bytes 15368 | tf_op jit(solution)/shard_map/ppermute | solution.py:23
  253.6 5.5 %collective-permute-start.26 = (f32[10,1,128]{2,1,0:T(1,128)S(1)}, f32[10,1,128]{2,1,0:T(1,128)S(1)}, u32[]{:S(2)}, u32[]{:S(2)}) collective-permute-start(f32[10,1,128]{2,1,0:T(1,128)S(1)} %get-tuple-element.118), channel_id=1, source_target_pairs={{1,0},{2,1},{3,2},{0,3},{5,4},{6,5},{7,6},{4,7},{9,8},{10,9},{11,1... | collective-permute-start | bytes 15368 | tf_op jit(solution)/shard_map/ppermute | solution.py:24
  259.3 22.3 %copy-start.1 = (f32[8,8,128]{2,1,0:T(8,128)}, f32[8,8,128]{2,1,0:T(8,128)S(1)}, u32[]{:S(2)}) copy-start(f32[8,8,128]{2,1,0:T(8,128)S(1)} %fusion.53) | copy-start | bytes 98308
  259.4 8.9 %collective-permute-start.28 = (f32[6,2,8,128]{3,2,1,0:T(8,128)S(1)}, f32[6,2,8,128]{3,2,1,0:T(8,128)S(1)}, u32[]{:S(2)}, u32[]{:S(2)}) collective-permute-start(f32[6,2,8,128]{3,2,1,0:T(8,128)S(1)} %get-tuple-element.82), channel_id=1, source_target_pairs={{0,4},{4,8},{8,12},{12,16},{16,20},{20,24},{24,28},{28,32},{32,36}... | collective-permute-start | bytes 147464 | tf_op jit(solution)/shard_map/ppermute | solution.py:23
  261.3 8.7 %collective-permute-start.29 = (f32[6,2,8,128]{3,2,1,0:T(8,128)S(1)}, f32[6,2,8,128]{3,2,1,0:T(8,128)S(1)}, u32[]{:S(2)}, u32[]{:S(2)}) collective-permute-start(f32[6,2,8,128]{3,2,1,0:T(8,128)S(1)} %get-tuple-element.83), channel_id=1, source_target_pairs={{4,0},{8,4},{12,8},{16,12},{20,16},{24,20},{28,24},{32,28},{36,32}... | collective-permute-start | bytes 147464 | tf_op jit(solution)/shard_map/ppermute | solution.py:24
  270.0 7.7 %collective-permute-start.30 = (f32[6,12,2,128]{3,2,1,0:T(2,128)S(1)}, f32[6,12,2,128]{3,2,1,0:T(2,128)S(1)}, u32[]{:S(2)}, u32[]{:S(2)}) collective-permute-start(f32[6,12,2,128]{3,2,1,0:T(2,128)S(1)} %get-tuple-element.77), channel_id=1, source_target_pairs={{0,1},{1,2},{2,3},{3,0},{4,5},{5,6},{6,7},{7,4},{8,9},{9,10},{10,1... | collective-permute-start | bytes 221192 | tf_op jit(solution)/shard_map/ppermute | solution.py:23
  274.0 6.2 %collective-permute-start.31 = (f32[6,12,2,128]{3,2,1,0:T(2,128)S(1)}, f32[6,12,2,128]{3,2,1,0:T(2,128)S(1)}, u32[]{:S(2)}, u32[]{:S(2)}) collective-permute-start(f32[6,12,2,128]{3,2,1,0:T(2,128)S(1)} %get-tuple-element.78), channel_id=1, source_target_pairs={{1,0},{2,1},{3,2},{0,3},{5,4},{6,5},{7,6},{4,7},{9,8},{10,9},{11,1... | collective-permute-start | bytes 221192 | tf_op jit(solution)/shard_map/ppermute | solution.py:24
  394.0 0.8 copy-start.3
  394.0 0.8 copy-start.4
  396.8 0.8 copy-start.6
  396.8 1.5 copy-start.2
  396.8 1.5 copy-start.5
  398.5 0.8 copy-start.7
  399.4 5.3 %collective-permute-start.33 = (f32[5,2,4,8,128]{4,3,2,1,0:T(8,128)S(1)}, f32[5,2,4,8,128]{4,3,2,1,0:T(8,128)S(1)}, u32[]{:S(2)}, u32[]{:S(2)}) collective-permute-start(f32[5,2,4,8,128]{4,3,2,1,0:T(8,128)S(1)} %bitcast.125), channel_id=1, source_target_pairs={{4,0},{8,4},{12,8},{16,12},{20,16},{24,20},{28,24},{32,28},{36,32}... | collective-permute-start | bytes 491528 | tf_op jit(solution)/shard_map/ppermute | solution.py:24
  401.4 10.0 %collective-permute-start.32 = (f32[5,2,4,8,128]{4,3,2,1,0:T(8,128)S(1)}, f32[5,2,4,8,128]{4,3,2,1,0:T(8,128)S(1)}, u32[]{:S(2)}, u32[]{:S(2)}) collective-permute-start(f32[5,2,4,8,128]{4,3,2,1,0:T(8,128)S(1)} %bitcast.126), channel_id=1, source_target_pairs={{0,4},{4,8},{8,12},{12,16},{16,20},{20,24},{24,28},{28,32},{32,36}... | collective-permute-start | bytes 491528 | tf_op jit(solution)/shard_map/ppermute | solution.py:23
where the time goes:
time: 414 us; the launch traced here: 413 us
  blocking collectives  227 us (55%)
  starting transfers between devices  132 us (32%)
  waiting for transfers between devices  31.4 us (8%)
  other arithmetic  13.2 us (3%)
  local copies, waits for them, and re-layouts  5.99 us (1%)
    psum x1, blocking collectives, shards(): total_mass = lax.psum(jnp.sum(density), ('box', 'grp'))  118 us
    pmax x1, blocking collectives, shards(): top_speed = lax.pmax(jnp.max(signal_speed(conserved_state)), ('box', 'grp'))  109 us
    ppermute x17, starting transfers between devices, with_halo(): after = lax.ppermute(first, axis, down)  88.9 us
    ppermute x17, starting transfers between devices, with_halo(): before = lax.ppermute(last, axis, up)  43.4 us
    ppermute x17, waiting for transfers between devices, with_halo(): after = lax.ppermute(first, axis, down)  24.7 us
  transfers between devices with their start and end apart: 34, of which 17 were waited for; matrix products, arithmetic and copies ran while one was open for 0% of the time, Pallas kernels for 0%

commit v1 on v0

v1 whole, which is shorter than its diff:
```python
import jax
import jax.numpy as jnp
from jax import lax
from jax.experimental import pallas as pl
from jax.experimental.pallas import tpu as pltpu
from jax.sharding import Mesh, PartitionSpec as P

GAMMA = 5.0 / 3.0
COURANT = 0.3
W = (2.0 / 3.0) / 6.0
BOX = ("y", "z", "c")
F32 = jnp.float32
CONST_GAIN = 40.0 / 9.0


def roll(value, shift, axis):
    return pltpu.roll(value, shift % value.shape[axis], axis)


def prim_of(rho, mx, my, mz, energy):
    inv = 1.0 / rho
    vx, vy, vz = mx * inv, my * inv, mz * inv
    kinetic = 0.5 * (mx * vx + my * vy + mz * vz)
    return rho, vx, vy, vz, (GAMMA - 1.0) * (energy - kinetic)


def half_slope(back, ahead):
    low = jnp.minimum(back, ahead)
    high = jnp.maximum(back, ahead)
    return 0.5 * (jnp.maximum(low, 0.0) + jnp.minimum(high, 0.0))


def side(state, normal):
    rho, pressure = state[0], state[4]
    vel = state[1:4]
    u = vel[normal]
    mom = [rho * v for v in vel]
    energy = pressure * 1.5 + 0.5 * (mom[0] * vel[0] + mom[1] * vel[1] + mom[2] * vel[2])
    flux = [mom[normal]] + [mom[normal] * v for v in vel] + [u * (energy + pressure)]
    flux[1 + normal] = flux[1 + normal] + pressure
    sound = jnp.sqrt(GAMMA * pressure / rho)
    return [rho] + mom + [energy], flux, u - sound, u + sound


def hll(left, right, normal):
    cons_l, flux_l, slow_l, fast_l = side(left, normal)
    cons_r, flux_r, slow_r, fast_r = side(right, normal)
    low = jnp.minimum(jnp.minimum(slow_l, slow_r), 0.0)
    high = jnp.maximum(jnp.maximum(fast_l, fast_r), 0.0)
    inv = 1.0 / (high - low)
    a = high * inv
    b = low * inv
    ab = high * b
    return [a * fl - b * fr + ab * (cr - cl) for fl, fr, cl, cr in zip(flux_l, flux_r, cons_l, cons_r)]


def pack_rows_kernel(ids, cs, out, loc):
    g = ids[1]
    count = out.shape[0]
    row = lax.broadcasted_iota(jnp.int32, (8, 128), 0)
    mass = jnp.zeros((8, 128), F32)
    speed = jnp.zeros((8, 128), F32)
    for p in range(8):
        vals = [cs[f, p] for f in range(5)]
        rho, vx, vy, vz, pressure = prim_of(*vals)
        top = jnp.maximum(jnp.maximum(jnp.abs(vx), jnp.abs(vy)), jnp.abs(vz))
        speed = jnp.maximum(speed, top + jnp.sqrt(GAMMA * pressure / rho))
        mass = mass + rho
        last = jnp.zeros((8, 128), F32)
        first = jnp.zeros((8, 128), F32)
        for k in range(4):
            mine = (row // 2) == k
            last = jnp.where(mine, roll(vals[k + 1], 2 * k - 6, 0), last)
            first = jnp.where(mine, roll(vals[k + 1], 2 * k, 0), first)
        for j in range(count):
            out[j, p] = vals[0]
            out[j, 8 + p] = jnp.where(lax.rem(j - g + count, count) == 1, last, first)
    tile = jnp.where(row < 4, jnp.sum(mass), jnp.max(speed))
    loc[...] = tile
    for j in range(count):
        out[j, 16] = tile


def pack_planes_kernel(ids, cs, rows, up1, dn1, up2, dn2, red):
    g = ids[1]
    count = rows.shape[0]
    for t in range(4):
        src = lax.rem(g + t, count)
        for p in range(8):
            tile = rows[src, p]
            up1[4 * p + t] = tile
            dn1[4 * p + t] = tile
            if p >= 4:
                up2[4 * (p - 4) + t] = tile
            else:
                dn2[4 * p + t] = tile
    for f in range(4):
        for p in range(2):
            up1[32 + 2 * f + p] = cs[f + 1, 6 + p]
            dn1[32 + 2 * f + p] = cs[f + 1, p]
    mass = rows[0, 16][0:1]
    speed = rows[0, 16][4:5]
    for j in range(1, count):
        mass = mass + rows[j, 16][0:1]
        speed = jnp.maximum(speed, rows[j, 16][4:5])
    lane = lax.broadcasted_iota(jnp.int32, (1, 128), 1)
    line = jnp.where(lane < 64, mass, speed)
    for j in range(red.shape[0]):
        red[j] = line


def fold_kernel(got, out):
    mass = got[0]
    speed = got[0]
    for j in range(1, got.shape[0]):
        mass = mass + got[j]
        speed = jnp.maximum(speed, got[j])
    lane = lax.broadcasted_iota(jnp.int32, (1, 128), 1)
    line = jnp.where(lane < 64, mass, speed)
    for j in range(out.shape[0]):
        out[j] = line


def main_kernel(ids, boxes, loc, cs, rows, up1, dn1, up2, dn2, phi_out, delta, send_up, send_dn,
                src, fine, coarse_src, coarse_a, coarse_b, grav, prims, halo):
    b, g = ids[0], ids[1]
    count = rows.shape[0]
    rho_loc = loc[0:1, :] * (1.0 / 8192.0)

    for t in range(4):
        own = lax.rem(g + t, count)
        at = pl.ds(8 * t, 8)
        for p in range(4):
            src[p, at, :] = 2.0 * (rho_loc - up2[4 * p + t])
            src[28 + p, at, :] = 2.0 * (rho_loc - dn2[4 * p + t])
        for p in range(8):
            src[4 + p, at, :] = 2.0 * (rho_loc - up1[4 * p + t])
            src[12 + p, at, :] = 2.0 * (rho_loc - rows[own, p])
            src[20 + p, at, :] = 2.0 * (rho_loc - dn1[4 * p + t])

    def beside(below, here, above, step):
        total = below + above
        total = total + (roll(here, step, 0) + roll(here, -step, 0))
        return total + (roll(here, step, 1) + roll(here, -step, 1))

    head = 2.0 * W - 6.0 * W * W
    for p in range(1, 31):
        s = src[p]
        fine[p] = head * s + (W * W) * beside(src[p - 1], s, src[p + 1], 1)

    def residue(p):
        v = fine[p]
        return src[p] - 6.0 * v + beside(fine[p - 1], v, fine[p + 1], 1)

    even_y = lax.broadcasted_iota(jnp.int32, (32, 128), 0) % 2 == 0
    even_z = lax.broadcasted_iota(jnp.int32, (32, 128), 1) % 2 == 0
    for c in range(14):
        r = residue(2 + 2 * c) + residue(3 + 2 * c)
        r = r + jnp.where(even_y, roll(r, -1, 0), roll(r, 1, 0))
        r = r + jnp.where(even_z, roll(r, -1, 1), roll(r, 1, 1))
        coarse_src[c] = 0.5 * r
    for c in range(1, 13):
        s = coarse_src[c]
        coarse_a[c] = head * s + (W * W) * beside(coarse_src[c - 1], s, coarse_src[c + 1], 2)

    def relax(ref, right, n, step):
        v = ref[n]
        return (1.0 / 3.0) * v + W * (right + beside(ref[n - 1], v, ref[n + 1], step))

    for c in range(2, 12):
        coarse_b[c] = relax(coarse_a, coarse_src[c], c, 2)
    for c in range(3, 11):
        corr = relax(coarse_b, coarse_src[c], c, 2)
        for p in (2 * c + 2, 2 * c + 3):
            if 9 <= p <= 22:
                fine[p] = fine[p] + corr
    for p in range(10, 22):
        coarse_a[p - 9] = relax(fine, src[p], p, 1)
    for p in range(11, 21):
        coarse_b[p - 10] = relax(coarse_a, src[p], p - 9, 1)
    for p in range(8):
        v = coarse_b[p + 2]
        phi_out[p] = v[0:8]
        grav[0, p] = 0.5 * (coarse_b[p + 1, 0:8, :] - coarse_b[p + 3, 0:8, :])
        grav[1, p] = 0.5 * (roll(v, 1, 0) - roll(v, -1, 0))[0:8]
        own_rows = v[0:8]
        grav[2, p] = 0.5 * (roll(own_rows, 1, 1) - roll(own_rows, -1, 1))

    def put(ref, n, vals):
        for f, v in enumerate(prim_of(*vals)):
            ref[f, n] = v

    for p in range(2):
        put(prims, p, [up1[4 * (6 + p)]] + [up1[32 + 2 * f + p] for f in range(4)])
        put(prims, 10 + p, [dn1[4 * p]] + [dn1[32 + 2 * f + p] for f in range(4)])
    row = lax.broadcasted_iota(jnp.int32, (8, 128), 0)
    nxt = lax.rem(g + 1, count)
    prv = lax.rem(g + count - 1, count)
    for p in range(8):
        put(prims, 2 + p, [cs[f, p] for f in range(5)])
        ahead, behind = rows[nxt, 8 + p], rows[prv, 8 + p]
        vals = [jnp.where(row < 4, rows[nxt, p], rows[prv, p])]
        for k in range(4):
            vals.append(jnp.where(row < 4, roll(ahead, -2 * k, 0), roll(behind, 6 - 2 * k, 0)))
        put(halo, p, vals)

    def face_x(n):
        states = []
        for m, sign in ((n, 1.0), (n + 1, -1.0)):
            out = []
            for f in range(5):
                mid = prims[f, m]
                out.append(mid + sign * half_slope(mid - prims[f, m - 1], prims[f, m + 1] - mid))
            states.append(out)
        return hll(states[0], states[1], 0)

    def roll_faces(vals, normal, axis):
        left, right = [], []
        for v in vals:
            diff = roll(v, -1, axis) - v
            slope = half_slope(roll(diff, 1, axis), diff)
            left.append(v + slope)
            right.append(roll(v - slope, -1, axis))
        flux = hll(left, right, normal)
        return [fl - roll(fl, 1, axis) for fl in flux]

    def plane(p, before):
        after = face_x(p + 2)
        balance = [x - y for x, y in zip(after, before)]
        here = [prims[f, p + 2] for f in range(5)]
        tall = [jnp.concatenate([here[f], halo[f, p]], axis=0) for f in range(5)]
        for f, v in enumerate(roll_faces(tall, 1, 0)):
            balance[f] = balance[f] + v[0:8]
        for f, v in enumerate(roll_faces(here, 2, 1)):
            balance[f] = balance[f] + v
        pulls = [grav[d, p] for d in range(3)]
        moms = [cs[d + 1, p] for d in range(3)]
        delta[0, p] = -balance[0]
        for d in range(3):
            delta[d + 1, p] = cs[0, p] * pulls[d] - balance[d + 1]
        delta[4, p] = (moms[0] * pulls[0] + moms[1] * pulls[1] + moms[2] * pulls[2]) - balance[4]
        return tuple(after)

    lax.fori_loop(0, 8, plane, tuple(face_x(1)))

    last = boxes.shape[0] // 2 - 1
    for side_owner, send in ((jnp.minimum(b + 1, last), send_up), (jnp.maximum(b - 1, 0), send_dn)):
        second = jnp.logical_or(boxes[2 * side_owner] == 2 * b + 1, boxes[2 * side_owner + 1] == 2 * b + 1)
        start = jnp.where(second, 4, 0)
        for f in range(5):
            for p in range(4):
                send[f, p] = cs[f, start + p]
                send[5 + f, p] = delta[f, start + p]


def final_kernel(ids, boxes, loc, got, cs, delta, phi, from_dn, from_up, out, potential, *, cells):
    b = ids[0]
    mass = got[0]
    speed = got[0]
    for j in range(1, got.shape[0]):
        mass = mass + got[j]
        speed = jnp.maximum(speed, got[j])
    mass = jnp.broadcast_to(mass[:, 0:1], (1, 128))
    speed = jnp.broadcast_to(speed[:, 64:65], (1, 128))
    shift = CONST_GAIN * (mass / cells - loc[0:1, :] * (1.0 / 8192.0))
    step = COURANT / speed
    for p in range(8):
        potential[p] = phi[p] + shift
    for slot in range(2):
        rel = boxes[2 * b + slot] - 2 * b

        @pl.when(rel < 0)
        def _():
            for f in range(5):
                for p in range(4):
                    out[f, 4 * slot + p] = from_dn[f, p] + step * from_dn[5 + f, p]

        @pl.when(rel > 1)
        def _():
            for f in range(5):
                for p in range(4):
                    out[f, 4 * slot + p] = from_up[f, p] + step * from_up[5 + f, p]

        @pl.when(jnp.logical_and(rel >= 0, rel <= 1))
        def _():
            start = 4 * jnp.clip(rel, 0, 1)
            for f in range(5):
                for p in range(4):
                    out[f, 4 * slot + p] = cs[f, start + p] + step * delta[f, start + p]


def call(kernel, outs, scalars, scratch, *args):
    shapes = [jax.ShapeDtypeStruct(s, F32) for s in outs]
    smem = pl.BlockSpec(memory_space=pltpu.SMEM)
    vmem = pl.BlockSpec(memory_space=pltpu.VMEM)
    return pl.pallas_call(
        kernel,
        out_shape=shapes,
        in_specs=[smem if i < scalars else vmem for i in range(len(args))],
        out_specs=[vmem] * len(outs),
        scratch_shapes=[pltpu.VMEM(s, F32) for s in scratch],
        compiler_params=pltpu.CompilerParams(vmem_limit_bytes=16 * 1024 * 1024),
    )(*args)


def shards(cs, boxes):
    ids = jnp.stack([lax.axis_index(BOX), lax.axis_index("x")]).astype(jnp.int32)
    n_box, n_grp = lax.axis_size(BOX), lax.axis_size("x")
    cells = float(cs[0].size * n_box * n_grp)

    def shift(value, by):
        return lax.ppermute(value, BOX, [(i, (i + by) % n_box) for i in range(n_box)])

    packed, loc = call(pack_rows_kernel, [(n_grp, 17, 8, 128), (8, 128)], 1, [], ids, cs)
    rows = lax.all_to_all(packed, "x", 0, 0, tiled=True)
    n_zc = lax.axis_size(("z", "c"))
    n_y = lax.axis_size("y")
    up1, dn1, up2, dn2, red = call(
        pack_planes_kernel,
        [(40, 8, 128), (40, 8, 128), (16, 8, 128), (16, 8, 128), (n_zc, 1, 128)],
        1, [], ids, cs, rows)
    up1, dn1, up2, dn2 = shift(up1, 1), shift(dn1, -1), shift(up2, 2), shift(dn2, -2)
    red = lax.all_to_all(red, ("z", "c"), 0, 0, tiled=True)
    red, boxes_late = lax.optimization_barrier((red, boxes))
    (red,) = call(fold_kernel, [(n_y, 1, 128)], 0, [], red)
    red = lax.all_to_all(red, "y", 0, 0, tiled=True)
    state = (5, 8, 8, 128)
    phi, delta, send_up, send_dn = call(
        main_kernel,
        [(8, 8, 128), state, (10, 4, 8, 128), (10, 4, 8, 128)],
        2,
        [(32, 32, 128), (32, 32, 128), (14, 32, 128), (14, 32, 128), (14, 32, 128),
         (3, 8, 8, 128), (5, 12, 8, 128), state],
        ids, boxes_late, loc, cs, rows, up1, dn1, up2, dn2)
    from_dn, from_up = shift(send_up, 1), shift(send_dn, -1)

    def last(*refs):
        final_kernel(*refs, cells=cells)

    return call(last, [state, (8, 8, 128)], 2, [], ids, boxes, loc, red, cs, delta, phi, from_dn, from_up)


def solution(mesh):
    n_box, n_grp = mesh.devices.shape
    parts = (8, n_box // 16, 2) if n_box % 16 == 0 else (2, n_box // 4, 2)
    fine_mesh = Mesh(mesh.devices.reshape(*parts, n_grp), ("y", "z", "c", "x"))
    return jax.shard_map(
        lambda a, b: tuple(shards(a, b)),
        mesh=fine_mesh,
        in_specs=(P(None, BOX, "x", None), P()),
        out_specs=(P(None, BOX, "x", None), P(BOX, "x", None)),
        check_vma=False,
    )
```

time: 414 us -> 81.3 us (0.20)
  the two profiles are of different devices: /device:TPU:32 before, /device:TPU:2 now
where the time goes in v1:
time: 81.3 us; the launch traced here: 80.9 us
  blocking collectives  42.9 us (53%)
  starting transfers between devices  28.3 us (35%)
  Pallas kernels  7.97 us (10%)
  local copies, waits for them, and re-layouts  0.93 us (1%)
    ppermute x6, starting transfers between devices, shift(): lax.ppermute(value, BOX, [(i, (i + by) % n_box) for i in range(n_box)])  28.3 us
    all_to_all x1, blocking collectives, shards(): rows = lax.all_to_all(packed, 'x', 0, 0, tiled=True)  17.2 us
    all_to_all x1, blocking collectives, shards(): red = lax.all_to_all(red, 'y', 0, 0, tiled=True)  12.9 us
    all_to_all x1, blocking collectives, shards(): red = lax.all_to_all(red, ('z', 'c'), 0, 0, tiled=True)  12.8 us
    pallas_call x5, Pallas kernels, call(): pl.pallas_call(kernel, out_shape=shapes, in_specs=[smem if i < scalars el...  7.97 us
  transfers between devices with their start and end apart: 6, of which 0 were waited for; matrix products, arithmetic and copies ran while one was open for 0% of the time, Pallas kernels for 0%

profile of v1, /device:TPU:2, one launch (start us, length us, event | category | flops | bytes accessed | tf_op | source)
XLA Modules:
  0.0 80.9 jit_solution(18404600534579763866)
XLA Ops:
  0.6 0.1 pad_add_fusion.ids.refs_0_
  0.7 0.0 copy-start
  0.7 0.9 %copy-done = f32[5,8,8,128]{3,2,1,0:T(8,128)S(1)} copy-done((f32[5,8,8,128]{3,2,1,0:T(8,128)S(1)}, f32[5,8,8,128]{3,2,1,0:T(8,128)}, u32[]{:S(2)}) %copy-start) | copy-done | bytes 163864
  1.6 0.7 shard_map.41
  2.4 17.2 %all_to_all.15.rows = f32[4,17,8,128]{3,2,1,0:T(8,128)S(1)} all-to-all(f32[4,17,8,128]{3,2,1,0:T(8,128)S(1)} %get-tuple-element.16), channel_id=1, replica_groups=mesh['y'=8,'z'=12,'c'=2,'x'=4] {'x'}, dimensions={0} | all-to-all | bytes 557056 | tf_op jit(solution)/shard_map/all_to_all | solution.py:315
  19.6 0.6 shard_map.42
  20.2 1.9 %collective-permute-start = (f32[40,8,128]{2,1,0:T(8,128)S(1)}, f32[40,8,128]{2,1,0:T(8,128)S(1)}, u32[]{:S(2)}, u32[]{:S(2)}) collective-permute-start(f32[40,8,128]{2,1,0:T(8,128)S(1)} %get-tuple-element.20), channel_id=1, source_target_pairs={{0,4},{4,8},{8,12},{12,16},{16,20},{20,24},{24,28},{28,32},{32,36}... | collective-permute-start | bytes 491528 | tf_op jit(solution)/shard_map/ppermute | solution.py:312
  22.1 8.3 %collective-permute-start.1 = (f32[40,8,128]{2,1,0:T(8,128)S(1)}, f32[40,8,128]{2,1,0:T(8,128)S(1)}, u32[]{:S(2)}, u32[]{:S(2)}) collective-permute-start(f32[40,8,128]{2,1,0:T(8,128)S(1)} %get-tuple-element.21), channel_id=1, source_target_pairs={{0,764},{4,0},{8,4},{12,8},{16,12},{20,16},{24,20},{28,24},{32,28}... | collective-permute-start | bytes 491528 | tf_op jit(solution)/shard_map/ppermute | solution.py:312
  30.4 1.9 %collective-permute-start.2 = (f32[16,8,128]{2,1,0:T(8,128)S(1)}, f32[16,8,128]{2,1,0:T(8,128)S(1)}, u32[]{:S(2)}, u32[]{:S(2)}) collective-permute-start(f32[16,8,128]{2,1,0:T(8,128)S(1)} %get-tuple-element.22), channel_id=1, source_target_pairs={{0,8},{4,12},{8,16},{12,20},{16,24},{20,28},{24,32},{28,36},{32,40... | collective-permute-start | bytes 196616 | tf_op jit(solution)/shard_map/ppermute | solution.py:312
  32.3 7.2 %collective-permute-start.3 = (f32[16,8,128]{2,1,0:T(8,128)S(1)}, f32[16,8,128]{2,1,0:T(8,128)S(1)}, u32[]{:S(2)}, u32[]{:S(2)}) collective-permute-start(f32[16,8,128]{2,1,0:T(8,128)S(1)} %get-tuple-element.23), channel_id=1, source_target_pairs={{0,760},{4,764},{8,0},{12,4},{16,8},{20,12},{24,16},{28,20},{32,24... | collective-permute-start | bytes 196616 | tf_op jit(solution)/shard_map/ppermute | solution.py:312
  39.6 0.0 copy-start.2
  39.6 12.8 %all_to_all.16.got = f32[24,1,128]{2,1,0:T(1,128)S(1)} all-to-all(f32[24,1,128]{2,1,0:T(1,128)S(1)} %get-tuple-element.17), channel_id=1, replica_groups=mesh['y'=8,'z'=12,'c'=2,'x'=4] {'z','c'}, dimensions={0} | all-to-all | bytes 24576 | tf_op jit(solution)/shard_map/all_to_all | solution.py:323
  52.4 0.0 collective-permute-done.2.up2
  52.4 0.0 collective-permute-done.3.dn2
  52.4 0.0 collective-permute-done.up1
  52.4 0.0 collective-permute-done.1.dn1
  52.4 0.0 copy-done.2
  52.4 0.0 copy-start.1
  52.4 5.3 %shard_map.44 = (f32[8,8,128]{2,1,0:T(8,128)S(1)}, f32[5,8,8,128]{3,2,1,0:T(8,128)S(1)}, f32[10,4,8,128]{3,2,1,0:T(8,128)S(1)}, f32[10,4,8,128]{3,2,1,0:T(8,128)S(1)}) custom-call(s32[2]{0:T(128)S(1)} %pad_add_fusion.ids.refs_0_, s32[384]{0:T(512)S(1)} %copy-done.2, f32[8,128]{1,0:T(8,128)S(1)} %get-tuple-element.15.loc.refs_2_, ...), custom_call_target="tpu_custom_call" | custom-call | tf_op jit(solution)/shard_map/pallas_call | solution.py:296
  57.7 1.9 %collective-permute-start.4 = (f32[10,4,8,128]{3,2,1,0:T(8,128)S(1)}, f32[10,4,8,128]{3,2,1,0:T(8,128)S(1)}, u32[]{:S(2)}, u32[]{:S(2)}) collective-permute-start(f32[10,4,8,128]{3,2,1,0:T(8,128)S(1)} %get-tuple-element.26), channel_id=1, source_target_pairs={{0,4},{4,8},{8,12},{12,16},{16,20},{20,24},{24,28},{28,32},{32,36}... | collective-permute-start | bytes 491528 | tf_op jit(solution)/shard_map/ppermute | solution.py:312
  59.7 7.0 %collective-permute-start.5 = (f32[10,4,8,128]{3,2,1,0:T(8,128)S(1)}, f32[10,4,8,128]{3,2,1,0:T(8,128)S(1)}, u32[]{:S(2)}, u32[]{:S(2)}) collective-permute-start(f32[10,4,8,128]{3,2,1,0:T(8,128)S(1)} %get-tuple-element.27), channel_id=1, source_target_pairs={{0,764},{4,0},{8,4},{12,8},{16,12},{20,16},{24,20},{28,24},{32,28}... | collective-permute-start | bytes 491528 | tf_op jit(solution)/shard_map/ppermute | solution.py:312
  66.7 12.9 %all_to_all.17.refs_3_ = f32[8,1,128]{2,1,0:T(1,128)S(1)} all-to-all(f32[8,1,128]{2,1,0:T(1,128)S(1)} %shard_map.43), channel_id=1, replica_groups=mesh['y'=8,'z'=12,'c'=2,'x'=4] {'y'}, dimensions={0} | all-to-all | bytes 8192 | tf_op jit(solution)/shard_map/all_to_all | solution.py:326
  79.5 0.0 collective-permute-done.4.refs_7_
  79.5 0.0 collective-permute-done.5.refs_8_
  79.5 0.0 copy-done.1
  79.5 1.4 %shard_map.45 = (f32[5,8,8,128]{3,2,1,0:T(8,128)}, f32[8,8,128]{2,1,0:T(8,128)}) custom-call(s32[2]{0:T(128)S(1)} %pad_add_fusion.ids.refs_0_, s32[384]{0:T(512)S(1)} %copy-done.2, f32[8,128]{1,0:T(8,128)S(1)} %get-tuple-element.15.loc.refs_2_, f32[8,1,128]{2,1,0:T(1,128)S(1)} %all_to_all.17.refs_3_, f32[5,8,8,128]{3,2,1,0:T(8,128)S(1)} %copy-done.1, ...), custom_call_target="tpu_custom_call" | custom-call | tf_op jit(solution)/shard_map/pallas_call | solution.py:296
  (1 shorter events, 0.0 us)
Async XLA Ops:
  0.7 0.9 %copy-start = (f32[5,8,8,128]{3,2,1,0:T(8,128)S(1)}, f32[5,8,8,128]{3,2,1,0:T(8,128)}, u32[]{:S(2)}) copy-start(f32[5,8,8,128]{3,2,1,0:T(8,128)} %refs_4_.1) | copy-start | bytes 491524
  20.2 32.3 %collective-permute-start = (f32[40,8,128]{2,1,0:T(8,128)S(1)}, f32[40,8,128]{2,1,0:T(8,128)S(1)}, u32[]{:S(2)}, u32[]{:S(2)}) collective-permute-start(f32[40,8,128]{2,1,0:T(8,128)S(1)} %get-tuple-element.20), channel_id=1, source_target_pairs={{0,4},{4,8},{8,12},{12,16},{16,20},{20,24},{24,28},{28,32},{32,36}... | collective-permute-start | bytes 491528 | tf_op jit(solution)/shard_map/ppermute | solution.py:312
  22.1 30.3 %collective-permute-start.1 = (f32[40,8,128]{2,1,0:T(8,128)S(1)}, f32[40,8,128]{2,1,0:T(8,128)S(1)}, u32[]{:S(2)}, u32[]{:S(2)}) collective-permute-start(f32[40,8,128]{2,1,0:T(8,128)S(1)} %get-tuple-element.21), channel_id=1, source_target_pairs={{0,764},{4,0},{8,4},{12,8},{16,12},{20,16},{24,20},{28,24},{32,28}... | collective-permute-start | bytes 491528 | tf_op jit(solution)/shard_map/ppermute | solution.py:312
  30.4 22.0 %collective-permute-start.2 = (f32[16,8,128]{2,1,0:T(8,128)S(1)}, f32[16,8,128]{2,1,0:T(8,128)S(1)}, u32[]{:S(2)}, u32[]{:S(2)}) collective-permute-start(f32[16,8,128]{2,1,0:T(8,128)S(1)} %get-tuple-element.22), channel_id=1, source_target_pairs={{0,8},{4,12},{8,16},{12,20},{16,24},{20,28},{24,32},{28,36},{32,40... | collective-permute-start | bytes 196616 | tf_op jit(solution)/shard_map/ppermute | solution.py:312
  32.3 20.1 %collective-permute-start.3 = (f32[16,8,128]{2,1,0:T(8,128)S(1)}, f32[16,8,128]{2,1,0:T(8,128)S(1)}, u32[]{:S(2)}, u32[]{:S(2)}) collective-permute-start(f32[16,8,128]{2,1,0:T(8,128)S(1)} %get-tuple-element.23), channel_id=1, source_target_pairs={{0,760},{4,764},{8,0},{12,4},{16,8},{20,12},{24,16},{28,20},{32,24... | collective-permute-start | bytes 196616 | tf_op jit(solution)/shard_map/ppermute | solution.py:312
  39.6 12.9 %copy-start.2 = (s32[384]{0:T(512)S(1)}, s32[384]{0:T(512)}, u32[]{:S(2)}) copy-start(s32[384]{0:T(512)} %refs_1_.1) | copy-start | bytes 4612
  52.4 27.1 %copy-start.1 = (f32[5,8,8,128]{3,2,1,0:T(8,128)S(1)}, f32[5,8,8,128]{3,2,1,0:T(8,128)}, u32[]{:S(2)}) copy-start(f32[5,8,8,128]{3,2,1,0:T(8,128)} %refs_4_.1) | copy-start | bytes 491524
  57.7 21.8 %collective-permute-start.4 = (f32[10,4,8,128]{3,2,1,0:T(8,128)S(1)}, f32[10,4,8,128]{3,2,1,0:T(8,128)S(1)}, u32[]{:S(2)}, u32[]{:S(2)}) collective-permute-start(f32[10,4,8,128]{3,2,1,0:T(8,128)S(1)} %get-tuple-element.26), channel_id=1, source_target_pairs={{0,4},{4,8},{8,12},{12,16},{16,20},{20,24},{24,28},{28,32},{32,36}... | collective-permute-start | bytes 491528 | tf_op jit(solution)/shard_map/ppermute | solution.py:312
  59.7 19.9 %collective-permute-start.5 = (f32[10,4,8,128]{3,2,1,0:T(8,128)S(1)}, f32[10,4,8,128]{3,2,1,0:T(8,128)S(1)}, u32[]{:S(2)}, u32[]{:S(2)}) collective-permute-start(f32[10,4,8,128]{3,2,1,0:T(8,128)S(1)} %get-tuple-element.27), channel_id=1, source_target_pairs={{0,764},{4,0},{8,4},{12,8},{16,12},{20,16},{24,20},{28,24},{32,28}... | collective-permute-start | bytes 491528 | tf_op jit(solution)/shard_map/ppermute | solution.py:312

commit v2 on v1

--- a/solution.py
+++ b/solution.py
@@ -54,55 +54,53 @@
     return [a * fl - b * fr + ab * (cr - cl) for fl, fr, cl, cr in zip(flux_l, flux_r, cons_l, cons_r)]
 
 
-def pack_rows_kernel(ids, cs, out, loc):
-    g = ids[1]
+def pack_rows_kernel(ids, chip, out, loc):
+    b, g = ids[0], ids[1]
+    core = lax.rem(b, 2)
     count = out.shape[0]
     row = lax.broadcasted_iota(jnp.int32, (8, 128), 0)
     mass = jnp.zeros((8, 128), F32)
     speed = jnp.zeros((8, 128), F32)
-    for p in range(8):
-        vals = [cs[f, p] for f in range(5)]
+    for p in range(16):
+        vals = [chip[p // 8, f, p % 8] for f in range(5)]
         rho, vx, vy, vz, pressure = prim_of(*vals)
         top = jnp.maximum(jnp.maximum(jnp.abs(vx), jnp.abs(vy)), jnp.abs(vz))
         speed = jnp.maximum(speed, top + jnp.sqrt(GAMMA * pressure / rho))
         mass = mass + rho
+        for j in range(count):
+            out[j, p] = rho
+    for p in range(8):
         last = jnp.zeros((8, 128), F32)
         first = jnp.zeros((8, 128), F32)
         for k in range(4):
             mine = (row // 2) == k
-            last = jnp.where(mine, roll(vals[k + 1], 2 * k - 6, 0), last)
-            first = jnp.where(mine, roll(vals[k + 1], 2 * k, 0), first)
+            val = chip[core, k + 1, p]
+            last = jnp.where(mine, roll(val, 2 * k - 6, 0), last)
+            first = jnp.where(mine, roll(val, 2 * k, 0), first)
         for j in range(count):
-            out[j, p] = vals[0]
-            out[j, 8 + p] = jnp.where(lax.rem(j - g + count, count) == 1, last, first)
+            out[j, 16 + p] = jnp.where(lax.rem(j - g + count, count) == 1, last, first)
     tile = jnp.where(row < 4, jnp.sum(mass), jnp.max(speed))
     loc[...] = tile
     for j in range(count):
-        out[j, 16] = tile
-
-
-def pack_planes_kernel(ids, cs, rows, up1, dn1, up2, dn2, red):
-    g = ids[1]
+        out[j, 24] = tile
+
+
+def pack_planes_kernel(ids, chip, rows, pair, red):
+    b, g = ids[0], ids[1]
+    core = lax.rem(b, 2)
     count = rows.shape[0]
     for t in range(4):
         src = lax.rem(g + t, count)
-        for p in range(8):
-            tile = rows[src, p]
-            up1[4 * p + t] = tile
-            dn1[4 * p + t] = tile
-            if p >= 4:
-                up2[4 * (p - 4) + t] = tile
-            else:
-                dn2[4 * p + t] = tile
+        for i in range(12):
+            pair[4 * i + t] = rows[src, 4 * core + i]
     for f in range(4):
         for p in range(2):
-            up1[32 + 2 * f + p] = cs[f + 1, 6 + p]
-            dn1[32 + 2 * f + p] = cs[f + 1, p]
-    mass = rows[0, 16][0:1]
-    speed = rows[0, 16][4:5]
+            pair[48 + 2 * f + p] = chip[core, f + 1, 6 * core + p]
+    mass = rows[0, 24][0:1]
+    speed = rows[0, 24][4:5]
     for j in range(1, count):
-        mass = mass + rows[j, 16][0:1]
-        speed = jnp.maximum(speed, rows[j, 16][4:5])
+        mass = mass + rows[j, 24][0:1]
+        speed = jnp.maximum(speed, rows[j, 24][4:5])
     lane = lax.broadcasted_iota(jnp.int32, (1, 128), 1)
     line = jnp.where(lane < 64, mass, speed)
     for j in range(red.shape[0]):
@@ -121,22 +119,22 @@
         out[j] = line
 
 
-def main_kernel(ids, boxes, loc, cs, rows, up1, dn1, up2, dn2, phi_out, delta, send_up, send_dn,
-                src, fine, coarse_src, coarse_a, coarse_b, grav, prims, halo):
+def main_kernel(ids, boxes, loc, chip, rows, pairs, phi_out, delta, send,
+                wide, fine, coarse_src, coarse_a, coarse_b, grav, prims, halo):
     b, g = ids[0], ids[1]
+    core = lax.rem(b, 2)
     count = rows.shape[0]
-    rho_loc = loc[0:1, :] * (1.0 / 8192.0)
+    rho_loc = loc[0:1, :] * (1.0 / 16384.0)
 
     for t in range(4):
         own = lax.rem(g + t, count)
         at = pl.ds(8 * t, 8)
-        for p in range(4):
-            src[p, at, :] = 2.0 * (rho_loc - up2[4 * p + t])
-            src[28 + p, at, :] = 2.0 * (rho_loc - dn2[4 * p + t])
-        for p in range(8):
-            src[4 + p, at, :] = 2.0 * (rho_loc - up1[4 * p + t])
-            src[12 + p, at, :] = 2.0 * (rho_loc - rows[own, p])
-            src[20 + p, at, :] = 2.0 * (rho_loc - dn1[4 * p + t])
+        for i in range(12):
+            wide[i, at, :] = 2.0 * (rho_loc - pairs[0, 4 * i + t])
+            wide[28 + i, at, :] = 2.0 * (rho_loc - pairs[1, 4 * i + t])
+        for p in range(16):
+            wide[12 + p, at, :] = 2.0 * (rho_loc - rows[own, p])
+    src = wide.at[pl.ds(8 * core, 32)]
 
     def beside(below, here, above, step):
         total = below + above
@@ -190,16 +188,19 @@
         for f, v in enumerate(prim_of(*vals)):
             ref[f, n] = v
 
+    other = 1 - core
     for p in range(2):
-        put(prims, p, [up1[4 * (6 + p)]] + [up1[32 + 2 * f + p] for f in range(4)])
-        put(prims, 10 + p, [dn1[4 * p]] + [dn1[32 + 2 * f + p] for f in range(4)])
+        put(prims, 10 * core + p,
+            [pairs[core, 40 * other + 4 * p]] + [pairs[core, 48 + 2 * f + p] for f in range(4)])
+        put(prims, 10 * other + p, [chip[other, f, 6 * core + p] for f in range(5)])
     row = lax.broadcasted_iota(jnp.int32, (8, 128), 0)
     nxt = lax.rem(g + 1, count)
     prv = lax.rem(g + count - 1, count)
     for p in range(8):
-        put(prims, 2 + p, [cs[f, p] for f in range(5)])
-        ahead, behind = rows[nxt, 8 + p], rows[prv, 8 + p]
-        vals = [jnp.where(row < 4, rows[nxt, p], rows[prv, p])]
+        put(prims, 2 + p, [chip[core, f, p] for f in range(5)])
+        ahead, behind = rows[nxt, 16 + p], rows[prv, 16 + p]
+        at = 8 * core + p
+        vals = [jnp.where(row < 4, rows[nxt, at], rows[prv, at])]
         for k in range(4):
             vals.append(jnp.where(row < 4, roll(ahead, -2 * k, 0), roll(behind, 6 - 2 * k, 0)))
         put(halo, p, vals)
@@ -234,27 +235,28 @@
         for f, v in enumerate(roll_faces(here, 2, 1)):
             balance[f] = balance[f] + v
         pulls = [grav[d, p] for d in range(3)]
-        moms = [cs[d + 1, p] for d in range(3)]
+        moms = [chip[core, d + 1, p] for d in range(3)]
         delta[0, p] = -balance[0]
         for d in range(3):
-            delta[d + 1, p] = cs[0, p] * pulls[d] - balance[d + 1]
+            delta[d + 1, p] = chip[core, 0, p] * pulls[d] - balance[d + 1]
         delta[4, p] = (moms[0] * pulls[0] + moms[1] * pulls[1] + moms[2] * pulls[2]) - balance[4]
         return tuple(after)
 
     lax.fori_loop(0, 8, plane, tuple(face_x(1)))
 
     last = boxes.shape[0] // 2 - 1
-    for side_owner, send in ((jnp.minimum(b + 1, last), send_up), (jnp.maximum(b - 1, 0), send_dn)):
-        second = jnp.logical_or(boxes[2 * side_owner] == 2 * b + 1, boxes[2 * side_owner + 1] == 2 * b + 1)
-        start = jnp.where(second, 4, 0)
-        for f in range(5):
-            for p in range(4):
-                send[f, p] = cs[f, start + p]
-                send[5 + f, p] = delta[f, start + p]
-
-
-def final_kernel(ids, boxes, loc, got, cs, delta, phi, from_dn, from_up, out, potential, *, cells):
+    owner = jnp.clip(b + 2 * core - 1, 0, last)
+    second = jnp.logical_or(boxes[2 * owner] == 2 * b + 1, boxes[2 * owner + 1] == 2 * b + 1)
+    start = jnp.where(second, 4, 0)
+    for f in range(5):
+        for p in range(4):
+            send[f, p] = chip[core, f, start + p]
+            send[5 + f, p] = delta[f, start + p]
+
+
+def final_kernel(ids, boxes, loc, got, chip, deltas, phi, came, out, potential, *, cells):
     b = ids[0]
+    core = lax.rem(b, 2)
     mass = got[0]
     speed = got[0]
     for j in range(1, got.shape[0]):
@@ -262,31 +264,27 @@
         speed = jnp.maximum(speed, got[j])
     mass = jnp.broadcast_to(mass[:, 0:1], (1, 128))
     speed = jnp.broadcast_to(speed[:, 64:65], (1, 128))
-    shift = CONST_GAIN * (mass / cells - loc[0:1, :] * (1.0 / 8192.0))
+    shift = CONST_GAIN * (mass / cells - loc[0:1, :] * (1.0 / 16384.0))
     step = COURANT / speed
     for p in range(8):
         potential[p] = phi[p] + shift
     for slot in range(2):
-        rel = boxes[2 * b + slot] - 2 * b
-
-        @pl.when(rel < 0)
+        place = boxes[2 * b + slot] - 2 * (b - core)
+        inside = jnp.logical_and(place >= 0, place <= 3)
+
+        @pl.when(inside)
+        def _():
+            near = jnp.clip(place, 0, 3)
+            half, start = near // 2, 4 * lax.rem(near, 2)
+            for f in range(5):
+                for p in range(4):
+                    out[f, 4 * slot + p] = chip[half, f, start + p] + step * deltas[half, f, start + p]
+
+        @pl.when(jnp.logical_not(inside))
         def _():
             for f in range(5):
                 for p in range(4):
-                    out[f, 4 * slot + p] = from_dn[f, p] + step * from_dn[5 + f, p]
-
-        @pl.when(rel > 1)
-        def _():
-            for f in range(5):
-                for p in range(4):
-                    out[f, 4 * slot + p] = from_up[f, p] + step * from_up[5 + f, p]
-
-        @pl.when(jnp.logical_and(rel >= 0, rel <= 1))
-        def _():
-            start = 4 * jnp.clip(rel, 0, 1)
-            for f in range(5):
-                for p in range(4):
-                    out[f, 4 * slot + p] = cs[f, start + p] + step * delta[f, start + p]
+                    out[f, 4 * slot + p] = came[f, p] + step * came[5 + f, p]
 
 
 def call(kernel, outs, scalars, scratch, *args):
@@ -306,38 +304,35 @@
 def shards(cs, boxes):
     ids = jnp.stack([lax.axis_index(BOX), lax.axis_index("x")]).astype(jnp.int32)
     n_box, n_grp = lax.axis_size(BOX), lax.axis_size("x")
+    n_z, n_y = lax.axis_size("z"), lax.axis_size("y")
     cells = float(cs[0].size * n_box * n_grp)
-
-    def shift(value, by):
-        return lax.ppermute(value, BOX, [(i, (i + by) % n_box) for i in range(n_box)])
-
-    packed, loc = call(pack_rows_kernel, [(n_grp, 17, 8, 128), (8, 128)], 1, [], ids, cs)
+    mates = [(i, (i + 2 * (i % 2) - 1) % n_box) for i in range(n_box)]
+
+    chip = lax.all_gather(cs, "c")
+    packed, loc = call(pack_rows_kernel, [(n_grp, 25, 8, 128), (8, 128)], 1, [], ids, chip)
     rows = lax.all_to_all(packed, "x", 0, 0, tiled=True)
-    n_zc = lax.axis_size(("z", "c"))
-    n_y = lax.axis_size("y")
-    up1, dn1, up2, dn2, red = call(
-        pack_planes_kernel,
-        [(40, 8, 128), (40, 8, 128), (16, 8, 128), (16, 8, 128), (n_zc, 1, 128)],
-        1, [], ids, cs, rows)
-    up1, dn1, up2, dn2 = shift(up1, 1), shift(dn1, -1), shift(up2, 2), shift(dn2, -2)
-    red = lax.all_to_all(red, ("z", "c"), 0, 0, tiled=True)
-    red, boxes_late = lax.optimization_barrier((red, boxes))
+    pair, red = call(pack_planes_kernel, [(56, 8, 128), (n_z, 1, 128)], 1, [], ids, chip, rows)
+    pair = lax.ppermute(pair, BOX, mates)
+    red = lax.all_to_all(red, "z", 0, 0, tiled=True)
+    red, pair = lax.optimization_barrier((red, pair))
+    pairs = lax.all_gather(pair, "c")
     (red,) = call(fold_kernel, [(n_y, 1, 128)], 0, [], red)
     red = lax.all_to_all(red, "y", 0, 0, tiled=True)
     state = (5, 8, 8, 128)
-    phi, delta, send_up, send_dn = call(
+    phi, delta, send = call(
         main_kernel,
-        [(8, 8, 128), state, (10, 4, 8, 128), (10, 4, 8, 128)],
+        [(8, 8, 128), state, (10, 4, 8, 128)],
         2,
-        [(32, 32, 128), (32, 32, 128), (14, 32, 128), (14, 32, 128), (14, 32, 128),
+        [(40, 32, 128), (32, 32, 128), (14, 32, 128), (14, 32, 128), (14, 32, 128),
          (3, 8, 8, 128), (5, 12, 8, 128), state],
-        ids, boxes_late, loc, cs, rows, up1, dn1, up2, dn2)
-    from_dn, from_up = shift(send_up, 1), shift(send_dn, -1)
+        ids, boxes, loc, chip, rows, pairs)
+    came = lax.ppermute(send, BOX, mates)
+    deltas = lax.all_gather(delta, "c")
 
     def last(*refs):
         final_kernel(*refs, cells=cells)
 
-    return call(last, [state, (8, 8, 128)], 2, [], ids, boxes, loc, red, cs, delta, phi, from_dn, from_up)
+    return call(last, [state, (8, 8, 128)], 2, [], ids, boxes, loc, red, chip, deltas, phi, came)
 
 
 def solution(mesh):

time: 81.3 us -> 71.2 us (0.88)
  the two profiles are of different devices: /device:TPU:2 before, /device:TPU:1 now
where the time goes in v2:
time: 71.2 us; the launch traced here: 70.9 us
  blocking collectives  47.6 us (67%)
  starting transfers between devices  9.48 us (13%)
  Pallas kernels  8.59 us (12%)
  waiting for transfers between devices  3.77 us (5%)
    all_to_all x1, blocking collectives, shards(): red = lax.all_to_all(red, 'z', 0, 0, tiled=True)  18.3 us
    all_gather x1, blocking collectives, shards(): chip = lax.all_gather(cs, 'c')  12.4 us
    all_to_all x1, blocking collectives, shards(): rows = lax.all_to_all(packed, 'x', 0, 0, tiled=True)  10.4 us
    pallas_call x5, Pallas kernels, call(): pl.pallas_call(kernel, out_shape=shapes, in_specs=[smem if i < scalars el...  8.59 us
    all_to_all x1, starting transfers between devices, shards(): red = lax.all_to_all(red, 'y', 0, 0, tiled=True)  5.11 us
    all_gather x1, blocking collectives, shards(): pairs = lax.all_gather(pair, 'c')  3.82 us
    all_to_all x1, waiting for transfers between devices, shards(): red = lax.all_to_all(red, 'y', 0, 0, tiled=True)  3.77 us
    all_gather x1, blocking collectives, shards(): deltas = lax.all_gather(delta, 'c')  2.68 us
  transfers between devices with their start and end apart: 3, of which 1 were waited for; matrix products, arithmetic and copies ran while one was open for 0% of the time, Pallas kernels for 1%

profile of v2, /device:TPU:1, one launch (start us, length us, event | category | flops | bytes accessed | tf_op | source)
XLA Modules:
  0.0 70.9 jit_solution(2243225241245136737)
XLA Ops:
  0.6 12.4 %all-gather = f32[10,8,8,128]{3,2,1,0:T(8,128)S(1)} all-gather(f32[5,8,8,128]{3,2,1,0:T(8,128)} %param.2), channel_id=2, replica_groups=mesh['y'=8,'z'=12,'c'=2,'x'=4] {'c'}, dimensions={0}, use_global_device_ids=true | all-gather | bytes 491520 | tf_op jit(solution)/shard_map/all_gather | solution.py:311
  13.0 0.1 pad_add_fusion.ids.refs_0_
  13.1 0.7 %shard_map.41 = (f32[4,25,8,128]{3,2,1,0:T(8,128)S(1)}, f32[8,128]{1,0:T(8,128)S(1)}) custom-call(s32[2]{0:T(128)S(1)} %pad_add_fusion.ids.refs_0_, f32[2,5,8,8,128]{4,3,2,1,0:T(8,128)S(1)} %bitcast.5), custom_call_target="tpu_custom_call" | custom-call | tf_op jit(solution)/shard_map/pallas_call | solution.py:294
  13.9 10.4 %all_to_all.15.rows = f32[4,25,8,128]{3,2,1,0:T(8,128)S(1)} all-to-all(f32[4,25,8,128]{3,2,1,0:T(8,128)S(1)} %get-tuple-element.12), channel_id=1, replica_groups=mesh['y'=8,'z'=12,'c'=2,'x'=4] {'x'}, dimensions={0} | all-to-all | bytes 819200 | tf_op jit(solution)/shard_map/all_to_all | solution.py:313
  24.2 0.6 shard_map.42
  24.8 1.9 %collective-permute-start = (f32[56,8,128]{2,1,0:T(8,128)S(1)}, f32[56,8,128]{2,1,0:T(8,128)S(1)}, u32[]{:S(2)}, u32[]{:S(2)}) collective-permute-start(f32[56,8,128]{2,1,0:T(8,128)S(1)} %get-tuple-element.14), channel_id=1, source_target_pairs={{0,764},{4,8},{8,4},{12,16},{16,12},{20,24},{24,20},{28,32},{32,28... | collective-permute-start | bytes 688136 | tf_op jit(solution)/shard_map/ppermute | solution.py:315
  26.7 18.3 %all_to_all.16.got = f32[12,1,128]{2,1,0:T(1,128)S(1)} all-to-all(f32[12,1,128]{2,1,0:T(1,128)S(1)} %get-tuple-element.13), channel_id=1, replica_groups=mesh['y'=8,'z'=12,'c'=2,'x'=4] {'z'}, dimensions={0} | all-to-all | bytes 12288 | tf_op jit(solution)/shard_map/all_to_all | solution.py:316
  45.0 0.0 collective-permute-done
  45.0 3.8 %all-gather.1 = f32[112,8,128]{2,1,0:T(8,128)S(1)} all-gather(f32[56,8,128]{2,1,0:T(8,128)S(1)} %collective-permute-done), channel_id=3, replica_groups=mesh['y'=8,'z'=12,'c'=2,'x'=4] {'c'}, dimensions={0}, use_global_device_ids=true | all-gather | bytes 688128 | tf_op jit(solution)/shard_map/all_gather | solution.py:318
  48.8 0.0 copy-start
  48.9 0.7 copy-done
  49.5 5.3 %shard_map.44 = (f32[8,8,128]{2,1,0:T(8,128)S(1)}, f32[5,8,8,128]{3,2,1,0:T(8,128)S(1)}, f32[10,4,8,128]{3,2,1,0:T(8,128)S(1)}) custom-call(s32[2]{0:T(128)S(1)} %pad_add_fusion.ids.refs_0_, s32[384]{0:T(512)S(1)} %copy-done, f32[8,128]{1,0:T(8,128)S(1)} %get-tuple-element.11.loc.refs_2_, f32[2,5,8,8,128]{4,3,2,1,0:T(8,128)S(1)} %bitcast.7, ...), custom_call_target="tpu_custom_call" | custom-call | tf_op jit(solution)/shard_map/pallas_call | solution.py:294
  54.9 2.4 %collective-permute-start.1 = (f32[10,4,8,128]{3,2,1,0:T(8,128)S(1)}, f32[10,4,8,128]{3,2,1,0:T(8,128)S(1)}, u32[]{:S(2)}, u32[]{:S(2)}) collective-permute-start(f32[10,4,8,128]{3,2,1,0:T(8,128)S(1)} %get-tuple-element.19), channel_id=1, source_target_pairs={{0,764},{4,8},{8,4},{12,16},{16,12},{20,24},{24,20},{28,32},{32,28... | collective-permute-start | bytes 491528 | tf_op jit(solution)/shard_map/ppermute | solution.py:329
  57.3 0.6 shard_map.43
  57.9 5.1 %all-to-all-start.2 = ((f32[8,1,128]{2,1,0:T(1,128)}), f32[8,1,128]{2,1,0:T(1,128)S(1)}, u32[]{:S(2)}, u32[]{:S(2)}) async-start(f32[8,1,128]{2,1,0:T(1,128)} %shard_map.43), calls=%async_computation.2 | async-start | bytes 8192 | tf_op jit(solution)/shard_map/all_to_all | solution.py:320
  63.0 2.7 %all-gather.2 = f32[10,8,8,128]{3,2,1,0:T(8,128)S(1)} all-gather(f32[5,8,8,128]{3,2,1,0:T(8,128)S(1)} %get-tuple-element.17), channel_id=4, replica_groups=mesh['y'=8,'z'=12,'c'=2,'x'=4] {'c'}, dimensions={0}, use_global_device_ids=true | all-gather | bytes 491520 | tf_op jit(solution)/shard_map/all_gather | solution.py:330
  65.7 3.8 %all-to-all-done.2.refs_3_ = f32[8,1,128]{2,1,0:T(1,128)S(1)} async-done(((f32[8,1,128]{2,1,0:T(1,128)}), f32[8,1,128]{2,1,0:T(1,128)S(1)}, u32[]{:S(2)}, u32[]{:S(2)}) %all-to-all-start.2) | async-done | bytes 4128 | tf_op jit(solution)/shard_map/all_to_all | solution.py:320
  69.5 0.0 collective-permute-done.1.refs_7_
  69.5 1.4 %shard_map.45 = (f32[5,8,8,128]{3,2,1,0:T(8,128)}, f32[8,8,128]{2,1,0:T(8,128)}) custom-call(s32[2]{0:T(128)S(1)} %pad_add_fusion.ids.refs_0_, s32[384]{0:T(512)S(1)} %copy-done, f32[8,128]{1,0:T(8,128)S(1)} %get-tuple-element.11.loc.refs_2_, f32[8,1,128]{2,1,0:T(1,128)S(1)} %all-to-all-done.2.refs_3_, f32[2,5,8,8,128]{4,3,2,1,0:T(8,128)S(1)} %bitcast.8, ...), custom_call_target="tpu_custom_call" | custom-call | tf_op jit(solution)/shard_map/pallas_call | solution.py:294
Async XLA Ops:
  24.8 20.2 %collective-permute-start = (f32[56,8,128]{2,1,0:T(8,128)S(1)}, f32[56,8,128]{2,1,0:T(8,128)S(1)}, u32[]{:S(2)}, u32[]{:S(2)}) collective-permute-start(f32[56,8,128]{2,1,0:T(8,128)S(1)} %get-tuple-element.14), channel_id=1, source_target_pairs={{0,764},{4,8},{8,4},{12,16},{16,12},{20,24},{24,20},{28,32},{32,28... | collective-permute-start | bytes 688136 | tf_op jit(solution)/shard_map/ppermute | solution.py:315
  48.8 0.7 copy-start
  54.9 14.6 %collective-permute-start.1 = (f32[10,4,8,128]{3,2,1,0:T(8,128)S(1)}, f32[10,4,8,128]{3,2,1,0:T(8,128)S(1)}, u32[]{:S(2)}, u32[]{:S(2)}) collective-permute-start(f32[10,4,8,128]{3,2,1,0:T(8,128)S(1)} %get-tuple-element.19), channel_id=1, source_target_pairs={{0,764},{4,8},{8,4},{12,16},{16,12},{20,24},{24,20},{28,32},{32,28... | collective-permute-start | bytes 491528 | tf_op jit(solution)/shard_map/ppermute | solution.py:329
  57.9 11.6 %all-to-all-start.2 = ((f32[8,1,128]{2,1,0:T(1,128)}), f32[8,1,128]{2,1,0:T(1,128)S(1)}, u32[]{:S(2)}, u32[]{:S(2)}) async-start(f32[8,1,128]{2,1,0:T(1,128)} %shard_map.43), calls=%async_computation.2 | async-start | bytes 8192 | tf_op jit(solution)/shard_map/all_to_all | solution.py:320

commit v3 on v2

--- a/solution.py
+++ b/solution.py
@@ -54,77 +54,83 @@
     return [a * fl - b * fr + ab * (cr - cl) for fl, fr, cl, cr in zip(flux_l, flux_r, cons_l, cons_r)]
 
 
-def pack_rows_kernel(ids, chip, out, loc):
-    b, g = ids[0], ids[1]
-    core = lax.rem(b, 2)
+def pack_rows_kernel(ids, cs, out, loc):
+    g = ids[1]
     count = out.shape[0]
     row = lax.broadcasted_iota(jnp.int32, (8, 128), 0)
     mass = jnp.zeros((8, 128), F32)
     speed = jnp.zeros((8, 128), F32)
-    for p in range(16):
-        vals = [chip[p // 8, f, p % 8] for f in range(5)]
+    for p in range(8):
+        vals = [cs[f, p] for f in range(5)]
         rho, vx, vy, vz, pressure = prim_of(*vals)
         top = jnp.maximum(jnp.maximum(jnp.abs(vx), jnp.abs(vy)), jnp.abs(vz))
         speed = jnp.maximum(speed, top + jnp.sqrt(GAMMA * pressure / rho))
         mass = mass + rho
-        for j in range(count):
-            out[j, p] = rho
-    for p in range(8):
         last = jnp.zeros((8, 128), F32)
         first = jnp.zeros((8, 128), F32)
         for k in range(4):
             mine = (row // 2) == k
-            val = chip[core, k + 1, p]
-            last = jnp.where(mine, roll(val, 2 * k - 6, 0), last)
-            first = jnp.where(mine, roll(val, 2 * k, 0), first)
+            last = jnp.where(mine, roll(vals[k + 1], 2 * k - 6, 0), last)
+            first = jnp.where(mine, roll(vals[k + 1], 2 * k, 0), first)
         for j in range(count):
-            out[j, 16 + p] = jnp.where(lax.rem(j - g + count, count) == 1, last, first)
+            out[j, p] = rho
+            out[j, 8 + p] = jnp.where(lax.rem(j - g + count, count) == 1, last, first)
     tile = jnp.where(row < 4, jnp.sum(mass), jnp.max(speed))
     loc[...] = tile
     for j in range(count):
-        out[j, 24] = tile
+        out[j, 16] = tile
 
 
 def pack_planes_kernel(ids, chip, rows, pair, red):
     b, g = ids[0], ids[1]
     core = lax.rem(b, 2)
-    count = rows.shape[0]
+    count = rows.shape[1]
     for t in range(4):
         src = lax.rem(g + t, count)
         for i in range(12):
-            pair[4 * i + t] = rows[src, 4 * core + i]
+            half = jnp.where(core == 0, i // 8, (4 + i) // 8)
+            place = jnp.where(core == 0, i % 8, (4 + i) % 8)
+            pair[4 * i + t] = rows[half, src, place]
     for f in range(4):
         for p in range(2):
             pair[48 + 2 * f + p] = chip[core, f + 1, 6 * core + p]
-    mass = rows[0, 24][0:1]
-    speed = rows[0, 24][4:5]
-    for j in range(1, count):
-        mass = mass + rows[j, 24][0:1]
-        speed = jnp.maximum(speed, rows[j, 24][4:5])
+    mass, speed = rows[0, 0, 16], rows[0, 0, 16]
+    for c in range(2):
+        for j in range(count):
+            if c + j > 0:
+                mass = mass + rows[c, j, 16]
+                speed = jnp.maximum(speed, rows[c, j, 16])
     lane = lax.broadcasted_iota(jnp.int32, (1, 128), 1)
-    line = jnp.where(lane < 64, mass, speed)
+    line = jnp.where(lane < 64, mass[0:1], speed[4:5])
     for j in range(red.shape[0]):
         red[j] = line
 
 
 def fold_kernel(got, out):
-    mass = got[0]
-    speed = got[0]
+    mass, speed = got[0], got[0]
     for j in range(1, got.shape[0]):
         mass = mass + got[j]
         speed = jnp.maximum(speed, got[j])
     lane = lax.broadcasted_iota(jnp.int32, (1, 128), 1)
-    line = jnp.where(lane < 64, mass, speed)
-    for j in range(out.shape[0]):
-        out[j] = line
-
-
-def main_kernel(ids, boxes, loc, chip, rows, pairs, phi_out, delta, send,
+    out[...] = jnp.broadcast_to(jnp.where(lane < 64, mass, speed), out.shape)
+
+
+def plan_kernel(ids, boxes, plan):
+    b = ids[0]
+    core = lax.rem(b, 2)
+    owner = jnp.clip(b + 2 * core - 1, 0, boxes.shape[0] // 2 - 1)
+    second = jnp.logical_or(boxes[2 * owner] == 2 * b + 1, boxes[2 * owner + 1] == 2 * b + 1)
+    plan[0] = jnp.where(second, 4, 0)
+    for slot in range(2):
+        plan[1 + slot] = boxes[2 * b + slot] - 2 * (b - core)
+
+
+def main_kernel(ids, plan, loc, chip, rows, pairs, phi_out, delta, send,
                 wide, fine, coarse_src, coarse_a, coarse_b, grav, prims, halo):
     b, g = ids[0], ids[1]
     core = lax.rem(b, 2)
-    count = rows.shape[0]
-    rho_loc = loc[0:1, :] * (1.0 / 16384.0)
+    count = rows.shape[1]
+    rho_loc = loc[0:1, :] * (1.0 / 8192.0)
 
     for t in range(4):
         own = lax.rem(g + t, count)
@@ -133,7 +139,7 @@
             wide[i, at, :] = 2.0 * (rho_loc - pairs[0, 4 * i + t])
             wide[28 + i, at, :] = 2.0 * (rho_loc - pairs[1, 4 * i + t])
         for p in range(16):
-            wide[12 + p, at, :] = 2.0 * (rho_loc - rows[own, p])
+            wide[12 + p, at, :] = 2.0 * (rho_loc - rows[p // 8, own, p % 8])
     src = wide.at[pl.ds(8 * core, 32)]
 
     def beside(below, here, above, step):
@@ -198,9 +204,8 @@
     prv = lax.rem(g + count - 1, count)
     for p in range(8):
         put(prims, 2 + p, [chip[core, f, p] for f in range(5)])
-        ahead, behind = rows[nxt, 16 + p], rows[prv, 16 + p]
-        at = 8 * core + p
-        vals = [jnp.where(row < 4, rows[nxt, at], rows[prv, at])]
+        ahead, behind = rows[core, nxt, 8 + p], rows[core, prv, 8 + p]
+        vals = [jnp.where(row < 4, rows[core, nxt, p], rows[core, prv, p])]
         for k in range(4):
             vals.append(jnp.where(row < 4, roll(ahead, -2 * k, 0), roll(behind, 6 - 2 * k, 0)))
         put(halo, p, vals)
@@ -240,36 +245,30 @@
         for d in range(3):
             delta[d + 1, p] = chip[core, 0, p] * pulls[d] - balance[d + 1]
         delta[4, p] = (moms[0] * pulls[0] + moms[1] * pulls[1] + moms[2] * pulls[2]) - balance[4]
-        return tuple(after)
-
-    lax.fori_loop(0, 8, plane, tuple(face_x(1)))
-
-    last = boxes.shape[0] // 2 - 1
-    owner = jnp.clip(b + 2 * core - 1, 0, last)
-    second = jnp.logical_or(boxes[2 * owner] == 2 * b + 1, boxes[2 * owner + 1] == 2 * b + 1)
-    start = jnp.where(second, 4, 0)
+        return after
+
+    face = face_x(1)
+    for p in range(8):
+        face = plane(p, face)
+
+    start = plan[0]
     for f in range(5):
         for p in range(4):
             send[f, p] = chip[core, f, start + p]
             send[5 + f, p] = delta[f, start + p]
 
 
-def final_kernel(ids, boxes, loc, got, chip, deltas, phi, came, out, potential, *, cells):
-    b = ids[0]
-    core = lax.rem(b, 2)
-    mass = got[0]
-    speed = got[0]
-    for j in range(1, got.shape[0]):
-        mass = mass + got[j]
-        speed = jnp.maximum(speed, got[j])
+def final_kernel(plan, loc, got, chip, deltas, phi, came, out, potential, *, cells):
+    mass = jnp.sum(got[...], axis=0, keepdims=True)
+    speed = jnp.max(got[...], axis=0, keepdims=True)
     mass = jnp.broadcast_to(mass[:, 0:1], (1, 128))
     speed = jnp.broadcast_to(speed[:, 64:65], (1, 128))
-    shift = CONST_GAIN * (mass / cells - loc[0:1, :] * (1.0 / 16384.0))
+    shift = CONST_GAIN * (mass / cells - loc[0:1, :] * (1.0 / 8192.0))
     step = COURANT / speed
     for p in range(8):
         potential[p] = phi[p] + shift
     for slot in range(2):
-        place = boxes[2 * b + slot] - 2 * (b - core)
+        place = plan[1 + slot]
         inside = jnp.logical_and(place >= 0, place <= 3)
 
         @pl.when(inside)
@@ -287,16 +286,19 @@
                     out[f, 4 * slot + p] = came[f, p] + step * came[5 + f, p]
 
 
-def call(kernel, outs, scalars, scratch, *args):
-    shapes = [jax.ShapeDtypeStruct(s, F32) for s in outs]
-    smem = pl.BlockSpec(memory_space=pltpu.SMEM)
-    vmem = pl.BlockSpec(memory_space=pltpu.VMEM)
+def call(kernel, outs, ins, scratch, *args):
+    spaces = {"s": pltpu.SMEM, "v": pltpu.VMEM, "h": pltpu.HBM}
+    shapes, out_specs = [], []
+    for shape in outs:
+        scalar = len(shape) == 1
+        shapes.append(jax.ShapeDtypeStruct(shape, jnp.int32 if scalar else F32))
+        out_specs.append(pl.BlockSpec(memory_space=pltpu.SMEM if scalar else pltpu.VMEM))
     return pl.pallas_call(
         kernel,
         out_shape=shapes,
-        in_specs=[smem if i < scalars else vmem for i in range(len(args))],
-        out_specs=[vmem] * len(outs),
-        scratch_shapes=[pltpu.VMEM(s, F32) for s in scratch],
+        in_specs=[pl.BlockSpec(memory_space=spaces[i]) for i in ins],
+        out_specs=out_specs,
+        scratch_shapes=scratch,
         compiler_params=pltpu.CompilerParams(vmem_limit_bytes=16 * 1024 * 1024),
     )(*args)
 
@@ -304,35 +306,41 @@
 def shards(cs, boxes):
     ids = jnp.stack([lax.axis_index(BOX), lax.axis_index("x")]).astype(jnp.int32)
     n_box, n_grp = lax.axis_size(BOX), lax.axis_size("x")
-    n_z, n_y = lax.axis_size("z"), lax.axis_size("y")
+    n_y, n_z = lax.axis_size("y"), lax.axis_size("z")
     cells = float(cs[0].size * n_box * n_grp)
     mates = [(i, (i + 2 * (i % 2) - 1) % n_box) for i in range(n_box)]
 
+    packed, loc = call(pack_rows_kernel, [(n_grp, 17, 8, 128), (8, 128)], "sv", [], ids, cs)
+    rows = lax.all_to_all(packed, "x", 0, 0, tiled=True)
     chip = lax.all_gather(cs, "c")
-    packed, loc = call(pack_rows_kernel, [(n_grp, 25, 8, 128), (8, 128)], 1, [], ids, chip)
-    rows = lax.all_to_all(packed, "x", 0, 0, tiled=True)
-    pair, red = call(pack_planes_kernel, [(56, 8, 128), (n_z, 1, 128)], 1, [], ids, chip, rows)
+    boxes, chip = lax.optimization_barrier((boxes, chip))
+    (plan,) = call(plan_kernel, [(3,)], "ss", [], ids, boxes)
+    rows, plan = lax.optimization_barrier((rows, plan))
+    rows = lax.all_gather(rows, "c")
+    pair, red = call(pack_planes_kernel, [(56, 8, 128), (n_z, 1, 128)], "svv", [], ids, chip, rows)
     pair = lax.ppermute(pair, BOX, mates)
     red = lax.all_to_all(red, "z", 0, 0, tiled=True)
-    red, pair = lax.optimization_barrier((red, pair))
     pairs = lax.all_gather(pair, "c")
-    (red,) = call(fold_kernel, [(n_y, 1, 128)], 0, [], red)
-    red = lax.all_to_all(red, "y", 0, 0, tiled=True)
     state = (5, 8, 8, 128)
+    sizes = [(40, 32, 128), (32, 32, 128), (14, 32, 128), (14, 32, 128), (14, 32, 128),
+             (3, 8, 8, 128), (5, 12, 8, 128), state]
     phi, delta, send = call(
         main_kernel,
         [(8, 8, 128), state, (10, 4, 8, 128)],
-        2,
-        [(40, 32, 128), (32, 32, 128), (14, 32, 128), (14, 32, 128), (14, 32, 128),
-         (3, 8, 8, 128), (5, 12, 8, 128), state],
-        ids, boxes, loc, chip, rows, pairs)
+        "ssvvvv",
+        [pltpu.VMEM(size, F32) for size in sizes],
+        ids, plan, loc, chip, rows, pairs)
+    send, red = lax.optimization_barrier((send, red))
+    (red,) = call(fold_kernel, [(n_y, 128)], "v", [], red)
+    red = lax.all_to_all(red.reshape(n_y, 1, 128), "y", 0, 0, tiled=True)
     came = lax.ppermute(send, BOX, mates)
     deltas = lax.all_gather(delta, "c")
 
     def last(*refs):
         final_kernel(*refs, cells=cells)
 
-    return call(last, [state, (8, 8, 128)], 2, [], ids, boxes, loc, red, chip, deltas, phi, came)
+    return call(last, [state, (8, 8, 128)], "svvvvvv", [],
+                plan, loc, red.reshape(n_y, 128), chip, deltas, phi, came)
 
 
 def solution(mesh):

time: 71.2 us -> 64.7 us (0.909)
  blocking collectives: 47.6 us -> 24.1 us
  starting transfers between devices: 9.48 us -> 25 us
  Pallas kernels: 8.59 us -> 9.38 us
    all_to_all x2 -> x0, blocking collectives: 28.7 us -> none  [the longest x1 18.3 us: shards(): red = lax.all_to_all(red, 'z', 0, 0, tiled=True)]
    all_to_all x1 -> x3, starting transfers between devices: 5.11 us -> 17.2 us  [the longest x1 8.27 us: shards(): red = lax.all_to_all(red, 'z', 0, 0, tiled=True)]
    all_gather x0 -> x1, blocking collectives: none -> 5.66 us  [shards(): rows = lax.all_gather(rows, 'c')]
    ppermute x1, starting transfers between devices: 2.45 us -> 5.96 us  [shards(): came = lax.ppermute(send, BOX, mates)]
    all_gather x1, blocking collectives: 12.4 us -> 10.8 us  [shards(): chip = lax.all_gather(cs, 'c')]
    all_gather x1, blocking collectives: 3.82 us -> 4.78 us  [shards(): pairs = lax.all_gather(pair, 'c')]
    pallas_call x5 -> x6, Pallas kernels: 8.59 us -> 9.38 us  [call(): pl.pallas_call(kernel, out_shape=shapes, in_specs=[pl.BlockSpec(memory_sp...]
    all_to_all x1 -> x3, waiting for transfers between devices: 3.77 us -> 4.05 us  [the longest x1 3.66 us: shards(): red = lax.all_to_all(red.reshape(n_y, 1, 128), 'y', 0, 0, tiled=True)]
  transfers between devices with their start and end apart: 3 -> 5, of which waited for: 1 -> 2; matrix products, arithmetic and copies ran while one was open for 0% -> 0% of each run, Pallas kernels for 1% -> 8%
where the time goes in v3:
time: 64.7 us; the launch traced here: 64.2 us
  starting transfers between devices  25 us (39%)
  blocking collectives  24.1 us (37%)
  Pallas kernels  9.38 us (14%)
  waiting for transfers between devices  4.06 us (6%)
  local copies, waits for them, and re-layouts  0.92 us (1%)
  between operations  0.71 us (1%)
    all_gather x1, blocking collectives, shards(): chip = lax.all_gather(cs, 'c')  10.8 us
    pallas_call x6, Pallas kernels, call(): pl.pallas_call(kernel, out_shape=shapes, in_specs=[pl.BlockSpec(memory_sp...  9.38 us
    all_to_all x1, starting transfers between devices, shards(): red = lax.all_to_all(red, 'z', 0, 0, tiled=True)  8.27 us
    ppermute x1, starting transfers between devices, shards(): came = lax.ppermute(send, BOX, mates)  5.96 us
    all_gather x1, blocking collectives, shards(): rows = lax.all_gather(rows, 'c')  5.66 us
    all_to_all x1, starting transfers between devices, shards(): rows = lax.all_to_all(packed, 'x', 0, 0, tiled=True)  4.97 us
    all_gather x1, blocking collectives, shards(): pairs = lax.all_gather(pair, 'c')  4.78 us
    all_to_all x1, starting transfers between devices, shards(): red = lax.all_to_all(red.reshape(n_y, 1, 128), 'y', 0, 0, tiled=True)  3.94 us
  transfers between devices with their start and end apart: 5, of which 2 were waited for; matrix products, arithmetic and copies ran while one was open for 0% of the time, Pallas kernels for 8%

profile of v3, /device:TPU:1, one launch (start us, length us, event | category | flops | bytes accessed | tf_op | source)
XLA Modules:
  0.0 64.2 jit_solution(15459313769818417617)
XLA Ops:
  0.6 0.1 pad_add_fusion.ids
  0.7 0.0 copy-start
  0.7 0.9 %copy-done = f32[5,8,8,128]{3,2,1,0:T(8,128)S(1)} copy-done((f32[5,8,8,128]{3,2,1,0:T(8,128)S(1)}, f32[5,8,8,128]{3,2,1,0:T(8,128)}, u32[]{:S(2)}) %copy-start) | copy-done | bytes 163864
  1.6 1.4 %shard_map.41 = (f32[4,17,8,128]{3,2,1,0:T(8,128)}, f32[8,128]{1,0:T(8,128)S(1)}) custom-call(s32[2]{0:T(128)S(1)} %pad_add_fusion.ids, f32[5,8,8,128]{3,2,1,0:T(8,128)S(1)} %copy-done), custom_call_target="tpu_custom_call" | custom-call | tf_op jit(solution)/shard_map/pallas_call | solution.py:296
  3.1 0.0 copy-start.1
  3.1 5.0 %all-to-all-start = ((f32[4,17,8,128]{3,2,1,0:T(8,128)}), f32[4,17,8,128]{3,2,1,0:T(8,128)S(1)}, u32[]{:S(2)}, u32[]{:S(2)}) async-start(f32[4,17,8,128]{3,2,1,0:T(8,128)} %get-tuple-element.15), calls=%async_computation | async-start | bytes 557056 | tf_op jit(solution)/shard_map/all_to_all | solution.py:314
  8.0 0.0 copy-done.1
  8.0 0.0 copy-start.2
  8.0 10.8 %all-gather = f32[10,8,8,128]{3,2,1,0:T(8,128)S(1)} all-gather(f32[5,8,8,128]{3,2,1,0:T(8,128)S(1)} %copy-done.1), channel_id=2, replica_groups=mesh['y'=8,'z'=12,'c'=2,'x'=4] {'c'}, dimensions={0}, use_global_device_ids=true | all-gather | bytes 491520 | tf_op jit(solution)/shard_map/all_gather | solution.py:315
  18.9 0.0 copy-done.2
  18.9 1.2 %shard_map.42.plan.refs_0_ = s32[3]{0:T(128)S(1)} custom-call(s32[2]{0:T(128)S(1)} %pad_add_fusion.ids, s32[384]{0:T(512)S(1)} %copy-done.2), custom_call_target="tpu_custom_call" | custom-call | tf_op jit(solution)/shard_map/pallas_call | solution.py:296
  20.1 0.0 all-to-all-done
  20.1 5.7 %all-gather.1 = f32[8,17,8,128]{3,2,1,0:T(8,128)S(1)} all-gather(f32[4,17,8,128]{3,2,1,0:T(8,128)S(1)} %all-to-all-done), channel_id=3, replica_groups=mesh['y'=8,'z'=12,'c'=2,'x'=4] {'c'}, dimensions={0}, use_global_device_ids=true | all-gather | bytes 835584 | tf_op jit(solution)/shard_map/all_gather | solution.py:319
  25.7 1.2 %shard_map.43 = (f32[56,8,128]{2,1,0:T(8,128)S(1)}, f32[12,1,128]{2,1,0:T(1,128)}) custom-call(s32[2]{0:T(128)S(1)} %pad_add_fusion.ids, f32[2,5,8,8,128]{4,3,2,1,0:T(8,128)S(1)} %bitcast.10, f32[2,4,17,8,128]{4,3,2,1,0:T(8,128)S(1)} %bitcast.13), custom_call_target="tpu_custom_call" | custom-call | tf_op jit(solution)/shard_map/pallas_call | solution.py:296
  26.9 1.9 %collective-permute-start = (f32[56,8,128]{2,1,0:T(8,128)S(1)}, f32[56,8,128]{2,1,0:T(8,128)S(1)}, u32[]{:S(2)}, u32[]{:S(2)}) collective-permute-start(f32[56,8,128]{2,1,0:T(8,128)S(1)} %get-tuple-element.21), channel_id=1, source_target_pairs={{0,764},{4,8},{8,4},{12,16},{16,12},{20,24},{24,20},{28,32},{32,28... | collective-permute-start | bytes 688136 | tf_op jit(solution)/shard_map/ppermute | solution.py:321
  28.8 8.3 %all-to-all-start.1 = ((f32[12,1,128]{2,1,0:T(1,128)}), f32[12,1,128]{2,1,0:T(1,128)S(1)}, u32[]{:S(2)}, u32[]{:S(2)}) async-start(f32[12,1,128]{2,1,0:T(1,128)} %get-tuple-element.23), calls=%async_computation.1 | async-start | bytes 12288 | tf_op jit(solution)/shard_map/all_to_all | solution.py:322
  37.1 0.0 collective-permute-done
  37.1 4.8 %all-gather.2 = f32[112,8,128]{2,1,0:T(8,128)S(1)} all-gather(f32[56,8,128]{2,1,0:T(8,128)S(1)} %collective-permute-done), channel_id=4, replica_groups=mesh['y'=8,'z'=12,'c'=2,'x'=4] {'c'}, dimensions={0}, use_global_device_ids=true | all-gather | bytes 688128 | tf_op jit(solution)/shard_map/all_gather | solution.py:323
  41.9 3.7 %shard_map.44 = (f32[8,8,128]{2,1,0:T(8,128)S(1)}, f32[5,8,8,128]{3,2,1,0:T(8,128)S(1)}, f32[10,4,8,128]{3,2,1,0:T(8,128)S(1)}) custom-call(s32[2]{0:T(128)S(1)} %pad_add_fusion.ids, s32[3]{0:T(128)S(1)} %shard_map.42.plan.refs_0_, f32[8,128]{1,0:T(8,128)S(1)} %get-tuple-element.18.loc.refs_1_, f32[2,5,8,8,128]{4,3,2,1,0:T(8,128)S(1)} %bitcast.11, ...), custom_call_target="tpu_custom_call" | custom-call | tf_op jit(solution)/shard_map/pallas_call | solution.py:296
  45.5 0.4 all-to-all-done.1.got
  45.9 6.0 %collective-permute-start.1 = (f32[10,4,8,128]{3,2,1,0:T(8,128)S(1)}, f32[10,4,8,128]{3,2,1,0:T(8,128)S(1)}, u32[]{:S(2)}, u32[]{:S(2)}) collective-permute-start(f32[10,4,8,128]{3,2,1,0:T(8,128)S(1)} %get-tuple-element.27), channel_id=1, source_target_pairs={{0,764},{4,8},{8,4},{12,16},{16,12},{20,24},{24,20},{28,32},{32,28... | collective-permute-start | bytes 491528 | tf_op jit(solution)/shard_map/ppermute | solution.py:336
  51.9 0.6 shard_map.45
  52.5 3.9 %all-to-all-start.2 = ((f32[8,1,128]{2,1,0:T(1,128)}), f32[8,1,128]{2,1,0:T(1,128)S(1)}, u32[]{:S(2)}, u32[]{:S(2)}) async-start(f32[8,1,128]{2,1,0:T(1,128)} %bitcast.6), calls=%async_computation.2 | async-start | bytes 8192 | tf_op jit(solution)/shard_map/all_to_all | solution.py:335
  56.5 2.8 %all-gather.3 = f32[10,8,8,128]{3,2,1,0:T(8,128)S(1)} all-gather(f32[5,8,8,128]{3,2,1,0:T(8,128)S(1)} %get-tuple-element.25), channel_id=5, replica_groups=mesh['y'=8,'z'=12,'c'=2,'x'=4] {'c'}, dimensions={0}, use_global_device_ids=true | all-gather | bytes 491520 | tf_op jit(solution)/shard_map/all_gather | solution.py:337
  59.3 3.7 %all-to-all-done.2 = f32[8,1,128]{2,1,0:T(1,128)S(1)} async-done(((f32[8,1,128]{2,1,0:T(1,128)}), f32[8,1,128]{2,1,0:T(1,128)S(1)}, u32[]{:S(2)}, u32[]{:S(2)}) %all-to-all-start.2) | async-done | bytes 4128 | tf_op jit(solution)/shard_map/all_to_all | solution.py:335
  62.9 0.0 collective-permute-done.1.refs_6_
  62.9 1.3 %shard_map.46 = (f32[5,8,8,128]{3,2,1,0:T(8,128)}, f32[8,8,128]{2,1,0:T(8,128)}) custom-call(s32[3]{0:T(128)S(1)} %shard_map.42.plan.refs_0_, f32[8,128]{1,0:T(8,128)S(1)} %get-tuple-element.18.loc.refs_1_, f32[8,128]{1,0:T(8,128)S(1)} %bitcast.17, f32[2,5,8,8,128]{4,3,2,1,0:T(8,128)S(1)} %bitcast.12, f32[2,5,8,8,128]{4,3,2,1,0:T(8,128)S(1)} %bitcast.16, ...), custom_call_target="tpu_custom_call" | custom-call | tf_op jit(solution)/shard_map/pallas_call | solution.py:296
Async XLA Ops:
  0.7 0.9 %copy-start = (f32[5,8,8,128]{3,2,1,0:T(8,128)S(1)}, f32[5,8,8,128]{3,2,1,0:T(8,128)}, u32[]{:S(2)}) copy-start(f32[5,8,8,128]{3,2,1,0:T(8,128)} %cs.1) | copy-start | bytes 491524
  3.1 5.0 %copy-start.1 = (f32[5,8,8,128]{3,2,1,0:T(8,128)S(1)}, f32[5,8,8,128]{3,2,1,0:T(8,128)}, u32[]{:S(2)}) copy-start(f32[5,8,8,128]{3,2,1,0:T(8,128)} %cs.1) | copy-start | bytes 491524
  3.1 17.0 %all-to-all-start = ((f32[4,17,8,128]{3,2,1,0:T(8,128)}), f32[4,17,8,128]{3,2,1,0:T(8,128)S(1)}, u32[]{:S(2)}, u32[]{:S(2)}) async-start(f32[4,17,8,128]{3,2,1,0:T(8,128)} %get-tuple-element.15), calls=%async_computation | async-start | bytes 557056 | tf_op jit(solution)/shard_map/all_to_all | solution.py:314
  8.0 10.8 %copy-start.2 = (s32[384]{0:T(512)S(1)}, s32[384]{0:T(512)}, u32[]{:S(2)}) copy-start(s32[384]{0:T(512)} %boxes) | copy-start | bytes 4612
  26.9 10.2 %collective-permute-start = (f32[56,8,128]{2,1,0:T(8,128)S(1)}, f32[56,8,128]{2,1,0:T(8,128)S(1)}, u32[]{:S(2)}, u32[]{:S(2)}) collective-permute-start(f32[56,8,128]{2,1,0:T(8,128)S(1)} %get-tuple-element.21), channel_id=1, source_target_pairs={{0,764},{4,8},{8,4},{12,16},{16,12},{20,24},{24,20},{28,32},{32,28... | collective-permute-start | bytes 688136 | tf_op jit(solution)/shard_map/ppermute | solution.py:321
  28.8 17.1 %all-to-all-start.1 = ((f32[12,1,128]{2,1,0:T(1,128)}), f32[12,1,128]{2,1,0:T(1,128)S(1)}, u32[]{:S(2)}, u32[]{:S(2)}) async-start(f32[12,1,128]{2,1,0:T(1,128)} %get-tuple-element.23), calls=%async_computation.1 | async-start | bytes 12288 | tf_op jit(solution)/shard_map/all_to_all | solution.py:322
  45.9 17.0 %collective-permute-start.1 = (f32[10,4,8,128]{3,2,1,0:T(8,128)S(1)}, f32[10,4,8,128]{3,2,1,0:T(8,128)S(1)}, u32[]{:S(2)}, u32[]{:S(2)}) collective-permute-start(f32[10,4,8,128]{3,2,1,0:T(8,128)S(1)} %get-tuple-element.27), channel_id=1, source_target_pairs={{0,764},{4,8},{8,4},{12,16},{16,12},{20,24},{24,20},{28,32},{32,28... | collective-permute-start | bytes 491528 | tf_op jit(solution)/shard_map/ppermute | solution.py:336
  52.5 10.4 %all-to-all-start.2 = ((f32[8,1,128]{2,1,0:T(1,128)}), f32[8,1,128]{2,1,0:T(1,128)S(1)}, u32[]{:S(2)}, u32[]{:S(2)}) async-start(f32[8,1,128]{2,1,0:T(1,128)} %bitcast.6), calls=%async_computation.2 | async-start | bytes 8192 | tf_op jit(solution)/shard_map/all_to_all | solution.py:335

commit v4 on v3

--- a/solution.py
+++ b/solution.py
@@ -86,7 +86,7 @@
     core = lax.rem(b, 2)
     count = rows.shape[1]
     for t in range(4):
-        src = lax.rem(g + t, count)
+        src = lax.rem(g + t + count - 1, count)
         for i in range(12):
             half = jnp.where(core == 0, i // 8, (4 + i) // 8)
             place = jnp.where(core == 0, i % 8, (4 + i) % 8)
@@ -103,14 +103,14 @@
     lane = lax.broadcasted_iota(jnp.int32, (1, 128), 1)
     line = jnp.where(lane < 64, mass[0:1], speed[4:5])
     for j in range(red.shape[0]):
-        red[j] = line
+        red[j] = jnp.broadcast_to(line, red.shape[1:])
 
 
 def fold_kernel(got, out):
-    mass, speed = got[0], got[0]
+    mass, speed = got[0, 0:1], got[0, 0:1]
     for j in range(1, got.shape[0]):
-        mass = mass + got[j]
-        speed = jnp.maximum(speed, got[j])
+        mass = mass + got[j, 0:1]
+        speed = jnp.maximum(speed, got[j, 0:1])
     lane = lax.broadcasted_iota(jnp.int32, (1, 128), 1)
     out[...] = jnp.broadcast_to(jnp.where(lane < 64, mass, speed), out.shape)
 
@@ -126,14 +126,14 @@
 
 
 def main_kernel(ids, plan, loc, chip, rows, pairs, phi_out, delta, send,
-                wide, fine, coarse_src, coarse_a, coarse_b, grav, prims, halo):
+                wide, fine, spread, paired, coarse_src, coarse_a, coarse_b, post_a, post_b, grav, prims, halo):
     b, g = ids[0], ids[1]
     core = lax.rem(b, 2)
     count = rows.shape[1]
     rho_loc = loc[0:1, :] * (1.0 / 8192.0)
 
     for t in range(4):
-        own = lax.rem(g + t, count)
+        own = lax.rem(g + t + count - 1, count)
         at = pl.ds(8 * t, 8)
         for i in range(12):
             wide[i, at, :] = 2.0 * (rho_loc - pairs[0, 4 * i + t])
@@ -149,46 +149,60 @@
 
     head = 2.0 * W - 6.0 * W * W
     for p in range(1, 31):
-        s = src[p]
-        fine[p] = head * s + (W * W) * beside(src[p - 1], s, src[p + 1], 1)
-
-    def residue(p):
-        v = fine[p]
-        return src[p] - 6.0 * v + beside(fine[p - 1], v, fine[p + 1], 1)
-
-    even_y = lax.broadcasted_iota(jnp.int32, (32, 128), 0) % 2 == 0
-    even_z = lax.broadcasted_iota(jnp.int32, (32, 128), 1) % 2 == 0
+        at = slice(0, 32) if 9 <= p <= 22 else slice(0, 24)
+        s = src[p, at]
+        fine[p, at] = head * s + (W * W) * beside(src[p - 1, at], s, src[p + 1, at], 1)
+
+    even = lax.broadcasted_iota(jnp.int32, (16, 128), 1) % 2 == 0
     for c in range(14):
-        r = residue(2 + 2 * c) + residue(3 + 2 * c)
-        r = r + jnp.where(even_y, roll(r, -1, 0), roll(r, 1, 0))
-        r = r + jnp.where(even_z, roll(r, -1, 1), roll(r, 1, 1))
-        coarse_src[c] = 0.5 * r
+        low, high = 2 + 2 * c, 3 + 2 * c
+        both = fine[low] + fine[high]
+        near = (src[low] + src[high]) - 5.0 * both + (fine[low - 1] + fine[high + 1])
+        evens, odds = pl.ds(32 * c, 16, stride=2), pl.ds(32 * c + 1, 16, stride=2)
+        spread[32 * c:32 * c + 32, :] = near + (roll(both, 1, 0) + roll(both, -1, 0))
+        paired[32 * c:32 * c + 32, :] = both
+        r = spread[evens, :] + spread[odds, :]
+        f = paired[evens, :] + paired[odds, :]
+        r = r + (roll(f, 1, 1) + roll(f, -1, 1))
+        coarse_src[c] = 0.5 * (r + jnp.where(even, roll(r, -1, 1), roll(r, 1, 1)))
+
+    def beside_coarse(below, here, above):
+        total = below + above
+        total = total + (roll(here, 1, 0) + roll(here, -1, 0))
+        return total + (roll(here, 2, 1) + roll(here, -2, 1))
+
     for c in range(1, 13):
         s = coarse_src[c]
-        coarse_a[c] = head * s + (W * W) * beside(coarse_src[c - 1], s, coarse_src[c + 1], 2)
-
-    def relax(ref, right, n, step):
-        v = ref[n]
-        return (1.0 / 3.0) * v + W * (right + beside(ref[n - 1], v, ref[n + 1], step))
+        coarse_a[c] = head * s + (W * W) * beside_coarse(coarse_src[c - 1], s, coarse_src[c + 1])
+
+    def relax_coarse(ref, c):
+        v = ref[c]
+        return (1.0 / 3.0) * v + W * (coarse_src[c] + beside_coarse(ref[c - 1], v, ref[c + 1]))
 
     for c in range(2, 12):
-        coarse_b[c] = relax(coarse_a, coarse_src[c], c, 2)
+        coarse_b[c] = relax_coarse(coarse_a, c)
     for c in range(3, 11):
-        corr = relax(coarse_b, coarse_src[c], c, 2)
+        corr = relax_coarse(coarse_b, c)
+        spread[pl.ds(32 * c, 16, stride=2), :] = corr
+        spread[pl.ds(32 * c + 1, 16, stride=2), :] = corr
         for p in (2 * c + 2, 2 * c + 3):
             if 9 <= p <= 22:
-                fine[p] = fine[p] + corr
+                fine[p, 0:24] = fine[p, 0:24] + spread[32 * c:32 * c + 24, :]
+
+    def relax(below, v, above, right):
+        return (1.0 / 3.0) * v + W * (right + beside(below, v, above, 1))
+
     for p in range(10, 22):
-        coarse_a[p - 9] = relax(fine, src[p], p, 1)
+        post_a[p - 10] = relax(fine[p - 1, 0:24], fine[p, 0:24], fine[p + 1, 0:24], src[p, 0:24])
     for p in range(11, 21):
-        coarse_b[p - 10] = relax(coarse_a, src[p], p - 9, 1)
-    for p in range(8):
-        v = coarse_b[p + 2]
-        phi_out[p] = v[0:8]
-        grav[0, p] = 0.5 * (coarse_b[p + 1, 0:8, :] - coarse_b[p + 3, 0:8, :])
-        grav[1, p] = 0.5 * (roll(v, 1, 0) - roll(v, -1, 0))[0:8]
-        own_rows = v[0:8]
-        grav[2, p] = 0.5 * (roll(own_rows, 1, 1) - roll(own_rows, -1, 1))
+        post_b[p - 11] = relax(post_a[p - 11], post_a[p - 10], post_a[p - 9], src[p, 0:24])
+    for p in range(8):
+        v = post_b[p + 1]
+        mine = v[8:16]
+        phi_out[p] = mine
+        grav[0, p] = 0.5 * (post_b[p, 8:16] - post_b[p + 2, 8:16])
+        grav[1, p] = 0.5 * (roll(v, 1, 0) - roll(v, -1, 0))[8:16]
+        grav[2, p] = 0.5 * (roll(mine, 1, 1) - roll(mine, -1, 1))
 
     def put(ref, n, vals):
         for f, v in enumerate(prim_of(*vals)):
@@ -197,7 +211,7 @@
     other = 1 - core
     for p in range(2):
         put(prims, 10 * core + p,
-            [pairs[core, 40 * other + 4 * p]] + [pairs[core, 48 + 2 * f + p] for f in range(4)])
+            [pairs[core, 40 * other + 4 * p + 1]] + [pairs[core, 48 + 2 * f + p] for f in range(4)])
         put(prims, 10 * other + p, [chip[other, f, 6 * core + p] for f in range(5)])
     row = lax.broadcasted_iota(jnp.int32, (8, 128), 0)
     nxt = lax.rem(g + 1, count)
@@ -317,12 +331,13 @@
     (plan,) = call(plan_kernel, [(3,)], "ss", [], ids, boxes)
     rows, plan = lax.optimization_barrier((rows, plan))
     rows = lax.all_gather(rows, "c")
-    pair, red = call(pack_planes_kernel, [(56, 8, 128), (n_z, 1, 128)], "svv", [], ids, chip, rows)
+    pair, red = call(pack_planes_kernel, [(56, 8, 128), (n_z, 8, 128)], "svv", [], ids, chip, rows)
     pair = lax.ppermute(pair, BOX, mates)
     red = lax.all_to_all(red, "z", 0, 0, tiled=True)
     pairs = lax.all_gather(pair, "c")
     state = (5, 8, 8, 128)
-    sizes = [(40, 32, 128), (32, 32, 128), (14, 32, 128), (14, 32, 128), (14, 32, 128),
+    sizes = [(40, 32, 128), (32, 32, 128), (448, 128), (448, 128), (14, 16, 128), (14, 16, 128), (14, 16, 128),
+             (12, 24, 128), (10, 24, 128),
              (3, 8, 8, 128), (5, 12, 8, 128), state]
     phi, delta, send = call(
         main_kernel,
@@ -330,7 +345,7 @@
         "ssvvvv",
         [pltpu.VMEM(size, F32) for size in sizes],
         ids, plan, loc, chip, rows, pairs)
-    send, red = lax.optimization_barrier((send, red))
+    delta, red = lax.optimization_barrier((delta, red))
     (red,) = call(fold_kernel, [(n_y, 128)], "v", [], red)
     red = lax.all_to_all(red.reshape(n_y, 1, 128), "y", 0, 0, tiled=True)
     came = lax.ppermute(send, BOX, mates)

time: 64.7 us -> 64.3 us (level)
  the two profiles are of different devices: /device:TPU:1 before, /device:TPU:2 now
where the time goes in v4:
time: 64.3 us; the launch traced here: 63.8 us
  starting transfers between devices  36.5 us (57%)
  Pallas kernels  9.12 us (14%)
  blocking collectives  8.5 us (13%)
  waiting for transfers between devices  8.02 us (12%)
  local copies, waits for them, and re-layouts  0.92 us (1%)
  between operations  0.7 us (1%)
    all_to_all x1, starting transfers between devices, shards(): rows = lax.all_to_all(packed, 'x', 0, 0, tiled=True)  13.1 us
    ppermute x1, starting transfers between devices, shards(): pair = lax.ppermute(pair, BOX, mates)  9.16 us
    pallas_call x6, Pallas kernels, call(): pl.pallas_call(kernel, out_shape=shapes, in_specs=[pl.BlockSpec(memory_sp...  9.12 us
    ppermute x1, starting transfers between devices, shards(): came = lax.ppermute(send, BOX, mates)  7.24 us
    all_to_all x1, waiting for transfers between devices, shards(): red = lax.all_to_all(red.reshape(n_y, 1, 128), 'y', 0, 0, tiled=True)  5.57 us
    all_to_all x1, starting transfers between devices, shards(): red = lax.all_to_all(red.reshape(n_y, 1, 128), 'y', 0, 0, tiled=True)  3.51 us
    all_to_all x1, starting transfers between devices, shards(): red = lax.all_to_all(red, 'z', 0, 0, tiled=True)  3.51 us
    all_gather x1, blocking collectives, shards(): rows = lax.all_gather(rows, 'c')  2.19 us
  transfers between devices with their start and end apart: 5, of which 3 were waited for; matrix products, arithmetic and copies ran while one was open for 0% of the time, Pallas kernels for 8%

profile of v4, /device:TPU:2, one launch (start us, length us, event | category | flops | bytes accessed | tf_op | source)
XLA Modules:
  0.0 63.8 jit_solution(13382341315982658262)
XLA Ops:
  0.6 0.1 pad_add_fusion.ids
  0.7 0.0 copy-start
  0.7 0.9 %copy-done = f32[5,8,8,128]{3,2,1,0:T(8,128)S(1)} copy-done((f32[5,8,8,128]{3,2,1,0:T(8,128)S(1)}, f32[5,8,8,128]{3,2,1,0:T(8,128)}, u32[]{:S(2)}) %copy-start) | copy-done | bytes 163864
  1.6 1.4 %shard_map.41 = (f32[4,17,8,128]{3,2,1,0:T(8,128)}, f32[8,128]{1,0:T(8,128)S(1)}) custom-call(s32[2]{0:T(128)S(1)} %pad_add_fusion.ids, f32[5,8,8,128]{3,2,1,0:T(8,128)S(1)} %copy-done), custom_call_target="tpu_custom_call" | custom-call | tf_op jit(solution)/shard_map/pallas_call | solution.py:310
  3.1 0.0 copy-start.1
  3.1 13.1 %all-to-all-start = ((f32[4,17,8,128]{3,2,1,0:T(8,128)}), f32[4,17,8,128]{3,2,1,0:T(8,128)S(1)}, u32[]{:S(2)}, u32[]{:S(2)}) async-start(f32[4,17,8,128]{3,2,1,0:T(8,128)} %get-tuple-element.15), calls=%async_computation | async-start | bytes 557056 | tf_op jit(solution)/shard_map/all_to_all | solution.py:328
  16.2 0.0 copy-done.1
  16.2 0.0 copy-start.2
  16.2 2.2 %all-gather = f32[10,8,8,128]{3,2,1,0:T(8,128)S(1)} all-gather(f32[5,8,8,128]{3,2,1,0:T(8,128)S(1)} %copy-done.1), channel_id=2, replica_groups=mesh['y'=8,'z'=12,'c'=2,'x'=4] {'c'}, dimensions={0}, use_global_device_ids=true | all-gather | bytes 491520 | tf_op jit(solution)/shard_map/all_gather | solution.py:329
  18.3 0.0 copy-done.2
  18.3 1.2 %shard_map.42.plan.refs_0_ = s32[3]{0:T(128)S(1)} custom-call(s32[2]{0:T(128)S(1)} %pad_add_fusion.ids, s32[384]{0:T(512)S(1)} %copy-done.2), custom_call_target="tpu_custom_call" | custom-call | tf_op jit(solution)/shard_map/pallas_call | solution.py:310
  19.5 2.0 %all-to-all-done = f32[4,17,8,128]{3,2,1,0:T(8,128)S(1)} async-done(((f32[4,17,8,128]{3,2,1,0:T(8,128)}), f32[4,17,8,128]{3,2,1,0:T(8,128)S(1)}, u32[]{:S(2)}, u32[]{:S(2)}) %all-to-all-start) | async-done | bytes 278560 | tf_op jit(solution)/shard_map/all_to_all | solution.py:328
  21.5 2.2 %all-gather.1 = f32[8,17,8,128]{3,2,1,0:T(8,128)S(1)} all-gather(f32[4,17,8,128]{3,2,1,0:T(8,128)S(1)} %all-to-all-done), channel_id=3, replica_groups=mesh['y'=8,'z'=12,'c'=2,'x'=4] {'c'}, dimensions={0}, use_global_device_ids=true | all-gather | bytes 835584 | tf_op jit(solution)/shard_map/all_gather | solution.py:333
  23.7 1.2 %shard_map.43 = (f32[56,8,128]{2,1,0:T(8,128)S(1)}, f32[12,8,128]{2,1,0:T(8,128)}) custom-call(s32[2]{0:T(128)S(1)} %pad_add_fusion.ids, f32[2,5,8,8,128]{4,3,2,1,0:T(8,128)S(1)} %bitcast.10, f32[2,4,17,8,128]{4,3,2,1,0:T(8,128)S(1)} %bitcast.13), custom_call_target="tpu_custom_call" | custom-call | tf_op jit(solution)/shard_map/pallas_call | solution.py:310
  24.9 9.2 %collective-permute-start = (f32[56,8,128]{2,1,0:T(8,128)S(1)}, f32[56,8,128]{2,1,0:T(8,128)S(1)}, u32[]{:S(2)}, u32[]{:S(2)}) collective-permute-start(f32[56,8,128]{2,1,0:T(8,128)S(1)} %get-tuple-element.21), channel_id=1, source_target_pairs={{0,764},{4,8},{8,4},{12,16},{16,12},{20,24},{24,20},{28,32},{32,28... | collective-permute-start | bytes 688136 | tf_op jit(solution)/shard_map/ppermute | solution.py:335
  34.0 3.5 %all-to-all-start.1 = ((f32[12,8,128]{2,1,0:T(8,128)}), f32[12,8,128]{2,1,0:T(8,128)S(1)}, u32[]{:S(2)}, u32[]{:S(2)}) async-start(f32[12,8,128]{2,1,0:T(8,128)} %get-tuple-element.23), calls=%async_computation.1 | async-start | bytes 98304 | tf_op jit(solution)/shard_map/all_to_all | solution.py:336
  37.6 0.5 collective-permute-done
  38.0 2.1 %all-gather.2 = f32[112,8,128]{2,1,0:T(8,128)S(1)} all-gather(f32[56,8,128]{2,1,0:T(8,128)S(1)} %collective-permute-done), channel_id=4, replica_groups=mesh['y'=8,'z'=12,'c'=2,'x'=4] {'c'}, dimensions={0}, use_global_device_ids=true | all-gather | bytes 688128 | tf_op jit(solution)/shard_map/all_gather | solution.py:337
  40.2 3.4 %shard_map.44 = (f32[8,8,128]{2,1,0:T(8,128)S(1)}, f32[5,8,8,128]{3,2,1,0:T(8,128)S(1)}, f32[10,4,8,128]{3,2,1,0:T(8,128)S(1)}) custom-call(s32[2]{0:T(128)S(1)} %pad_add_fusion.ids, s32[3]{0:T(128)S(1)} %shard_map.42.plan.refs_0_, f32[8,128]{1,0:T(8,128)S(1)} %get-tuple-element.18.loc.refs_1_, f32[2,5,8,8,128]{4,3,2,1,0:T(8,128)S(1)} %bitcast.11, ...), custom_call_target="tpu_custom_call" | custom-call | tf_op jit(solution)/shard_map/pallas_call | solution.py:310
  43.5 7.2 %collective-permute-start.1 = (f32[10,4,8,128]{3,2,1,0:T(8,128)S(1)}, f32[10,4,8,128]{3,2,1,0:T(8,128)S(1)}, u32[]{:S(2)}, u32[]{:S(2)}) collective-permute-start(f32[10,4,8,128]{3,2,1,0:T(8,128)S(1)} %get-tuple-element.27), channel_id=1, source_target_pairs={{0,764},{4,8},{8,4},{12,16},{16,12},{20,24},{24,20},{28,32},{32,28... | collective-permute-start | bytes 491528 | tf_op jit(solution)/shard_map/ppermute | solution.py:351
  50.8 0.0 all-to-all-done.1.got
  50.8 0.6 shard_map.45
  51.4 3.5 %all-to-all-start.2 = ((f32[8,1,128]{2,1,0:T(1,128)}), f32[8,1,128]{2,1,0:T(1,128)S(1)}, u32[]{:S(2)}, u32[]{:S(2)}) async-start(f32[8,1,128]{2,1,0:T(1,128)} %bitcast.6), calls=%async_computation.2 | async-start | bytes 8192 | tf_op jit(solution)/shard_map/all_to_all | solution.py:350
  54.9 2.0 %all-gather.3 = f32[10,8,8,128]{3,2,1,0:T(8,128)S(1)} all-gather(f32[5,8,8,128]{3,2,1,0:T(8,128)S(1)} %get-tuple-element.25), channel_id=5, replica_groups=mesh['y'=8,'z'=12,'c'=2,'x'=4] {'c'}, dimensions={0}, use_global_device_ids=true | all-gather | bytes 491520 | tf_op jit(solution)/shard_map/all_gather | solution.py:352
  56.9 5.6 %all-to-all-done.2 = f32[8,1,128]{2,1,0:T(1,128)S(1)} async-done(((f32[8,1,128]{2,1,0:T(1,128)}), f32[8,1,128]{2,1,0:T(1,128)S(1)}, u32[]{:S(2)}, u32[]{:S(2)}) %all-to-all-start.2) | async-done | bytes 4128 | tf_op jit(solution)/shard_map/all_to_all | solution.py:350
  62.5 0.0 collective-permute-done.1.refs_6_
  62.5 1.3 %shard_map.46 = (f32[5,8,8,128]{3,2,1,0:T(8,128)}, f32[8,8,128]{2,1,0:T(8,128)}) custom-call(s32[3]{0:T(128)S(1)} %shard_map.42.plan.refs_0_, f32[8,128]{1,0:T(8,128)S(1)} %get-tuple-element.18.loc.refs_1_, f32[8,128]{1,0:T(8,128)S(1)} %bitcast.17, f32[2,5,8,8,128]{4,3,2,1,0:T(8,128)S(1)} %bitcast.12, f32[2,5,8,8,128]{4,3,2,1,0:T(8,128)S(1)} %bitcast.16, ...), custom_call_target="tpu_custom_call" | custom-call | tf_op jit(solution)/shard_map/pallas_call | solution.py:310
Async XLA Ops:
  0.7 0.9 %copy-start = (f32[5,8,8,128]{3,2,1,0:T(8,128)S(1)}, f32[5,8,8,128]{3,2,1,0:T(8,128)}, u32[]{:S(2)}) copy-start(f32[5,8,8,128]{3,2,1,0:T(8,128)} %cs.1) | copy-start | bytes 491524
  3.1 13.1 %copy-start.1 = (f32[5,8,8,128]{3,2,1,0:T(8,128)S(1)}, f32[5,8,8,128]{3,2,1,0:T(8,128)}, u32[]{:S(2)}) copy-start(f32[5,8,8,128]{3,2,1,0:T(8,128)} %cs.1) | copy-start | bytes 491524
  3.1 18.4 %all-to-all-start = ((f32[4,17,8,128]{3,2,1,0:T(8,128)}), f32[4,17,8,128]{3,2,1,0:T(8,128)S(1)}, u32[]{:S(2)}, u32[]{:S(2)}) async-start(f32[4,17,8,128]{3,2,1,0:T(8,128)} %get-tuple-element.15), calls=%async_computation | async-start | bytes 557056 | tf_op jit(solution)/shard_map/all_to_all | solution.py:328
  16.2 2.2 %copy-start.2 = (s32[384]{0:T(512)S(1)}, s32[384]{0:T(512)}, u32[]{:S(2)}) copy-start(s32[384]{0:T(512)} %boxes) | copy-start | bytes 4612
  24.9 13.2 %collective-permute-start = (f32[56,8,128]{2,1,0:T(8,128)S(1)}, f32[56,8,128]{2,1,0:T(8,128)S(1)}, u32[]{:S(2)}, u32[]{:S(2)}) collective-permute-start(f32[56,8,128]{2,1,0:T(8,128)S(1)} %get-tuple-element.21), channel_id=1, source_target_pairs={{0,764},{4,8},{8,4},{12,16},{16,12},{20,24},{24,20},{28,32},{32,28... | collective-permute-start | bytes 688136 | tf_op jit(solution)/shard_map/ppermute | solution.py:335
  34.0 16.7 %all-to-all-start.1 = ((f32[12,8,128]{2,1,0:T(8,128)}), f32[12,8,128]{2,1,0:T(8,128)S(1)}, u32[]{:S(2)}, u32[]{:S(2)}) async-start(f32[12,8,128]{2,1,0:T(8,128)} %get-tuple-element.23), calls=%async_computation.1 | async-start | bytes 98304 | tf_op jit(solution)/shard_map/all_to_all | solution.py:336
  43.5 19.0 %collective-permute-start.1 = (f32[10,4,8,128]{3,2,1,0:T(8,128)S(1)}, f32[10,4,8,128]{3,2,1,0:T(8,128)S(1)}, u32[]{:S(2)}, u32[]{:S(2)}) collective-permute-start(f32[10,4,8,128]{3,2,1,0:T(8,128)S(1)} %get-tuple-element.27), channel_id=1, source_target_pairs={{0,764},{4,8},{8,4},{12,16},{16,12},{20,24},{24,20},{28,32},{32,28... | collective-permute-start | bytes 491528 | tf_op jit(solution)/shard_map/ppermute | solution.py:351
  51.4 11.1 %all-to-all-start.2 = ((f32[8,1,128]{2,1,0:T(1,128)}), f32[8,1,128]{2,1,0:T(1,128)S(1)}, u32[]{:S(2)}, u32[]{:S(2)}) async-start(f32[8,1,128]{2,1,0:T(1,128)} %bitcast.6), calls=%async_computation.2 | async-start | bytes 8192 | tf_op jit(solution)/shard_map/all_to_all | solution.py:350

commit v5 on v4

--- a/solution.py
+++ b/solution.py
@@ -115,7 +115,34 @@
     out[...] = jnp.broadcast_to(jnp.where(lane < 64, mass, speed), out.shape)
 
 
-def plan_kernel(ids, boxes, plan):
+def put(ref, n, vals):
+    for f, v in enumerate(prim_of(*vals)):
+        ref[f, n] = v
+
+
+def face_x(prims, n):
+    states = []
+    for m, sign in ((n + 1, 1.0), (n + 2, -1.0)):
+        out = []
+        for f in range(5):
+            mid = prims[f, m]
+            out.append(mid + sign * half_slope(mid - prims[f, m - 1], prims[f, m + 1] - mid))
+        states.append(out)
+    return hll(states[0], states[1], 0)
+
+
+def roll_faces(vals, normal, axis):
+    left, right = [], []
+    for v in vals:
+        diff = roll(v, -1, axis) - v
+        slope = half_slope(roll(diff, 1, axis), diff)
+        left.append(v + slope)
+        right.append(roll(v - slope, -1, axis))
+    flux = hll(left, right, normal)
+    return [fl - roll(fl, 1, axis) for fl in flux]
+
+
+def plan_kernel(ids, boxes, chip, plan, inner, third, prims):
     b = ids[0]
     core = lax.rem(b, 2)
     owner = jnp.clip(b + 2 * core - 1, 0, boxes.shape[0] // 2 - 1)
@@ -123,9 +150,20 @@
     plan[0] = jnp.where(second, 4, 0)
     for slot in range(2):
         plan[1 + slot] = boxes[2 * b + slot] - 2 * (b - core)
-
-
-def main_kernel(ids, plan, loc, chip, rows, pairs, phi_out, delta, send,
+    other = 1 - core
+    for p in range(8):
+        put(prims, 2 + p, [chip[core, f, p] for f in range(5)])
+    for p in range(2):
+        put(prims, 10 * other + p, [chip[other, f, 6 * core + p] for f in range(5)])
+    for k in range(7):
+        for f, v in enumerate(face_x(prims, 2 * other + k)):
+            inner[f, 2 * other + k] = v
+    for p in range(8):
+        for f, v in enumerate(roll_faces([prims[f, p + 2] for f in range(5)], 2, 1)):
+            third[f, p] = v
+
+
+def main_kernel(ids, plan, loc, chip, rows, inner, third, pairs, phi_out, delta, send,
                 wide, fine, spread, paired, coarse_src, coarse_a, coarse_b, post_a, post_b, grav, prims, halo):
     b, g = ids[0], ids[1]
     core = lax.rem(b, 2)
@@ -204,15 +242,10 @@
         grav[1, p] = 0.5 * (roll(v, 1, 0) - roll(v, -1, 0))[8:16]
         grav[2, p] = 0.5 * (roll(mine, 1, 1) - roll(mine, -1, 1))
 
-    def put(ref, n, vals):
-        for f, v in enumerate(prim_of(*vals)):
-            ref[f, n] = v
-
     other = 1 - core
     for p in range(2):
         put(prims, 10 * core + p,
             [pairs[core, 40 * other + 4 * p + 1]] + [pairs[core, 48 + 2 * f + p] for f in range(4)])
-        put(prims, 10 * other + p, [chip[other, f, 6 * core + p] for f in range(5)])
     row = lax.broadcasted_iota(jnp.int32, (8, 128), 0)
     nxt = lax.rem(g + 1, count)
     prv = lax.rem(g + count - 1, count)
@@ -224,35 +257,23 @@
             vals.append(jnp.where(row < 4, roll(ahead, -2 * k, 0), roll(behind, 6 - 2 * k, 0)))
         put(halo, p, vals)
 
-    def face_x(n):
-        states = []
-        for m, sign in ((n, 1.0), (n + 1, -1.0)):
-            out = []
-            for f in range(5):
-                mid = prims[f, m]
-                out.append(mid + sign * half_slope(mid - prims[f, m - 1], prims[f, m + 1] - mid))
-            states.append(out)
-        return hll(states[0], states[1], 0)
-
-    def roll_faces(vals, normal, axis):
-        left, right = [], []
-        for v in vals:
-            diff = roll(v, -1, axis) - v
-            slope = half_slope(roll(diff, 1, axis), diff)
-            left.append(v + slope)
-            right.append(roll(v - slope, -1, axis))
-        flux = hll(left, right, normal)
-        return [fl - roll(fl, 1, axis) for fl in flux]
+    outer = [face_x(prims, 7 * core + k) for k in range(2)]
+
+    def face(n):
+        known = [inner[f, n] for f in range(5)]
+        if n < 2:
+            return [jnp.where(core == 0, o, k) for o, k in zip(outer[n], known)]
+        if n > 6:
+            return [jnp.where(core == 1, o, k) for o, k in zip(outer[n - 7], known)]
+        return known
 
     def plane(p, before):
-        after = face_x(p + 2)
-        balance = [x - y for x, y in zip(after, before)]
+        after = face(p + 1)
+        balance = [x - y + third[f, p] for f, (x, y) in enumerate(zip(after, before))]
         here = [prims[f, p + 2] for f in range(5)]
         tall = [jnp.concatenate([here[f], halo[f, p]], axis=0) for f in range(5)]
         for f, v in enumerate(roll_faces(tall, 1, 0)):
             balance[f] = balance[f] + v[0:8]
-        for f, v in enumerate(roll_faces(here, 2, 1)):
-            balance[f] = balance[f] + v
         pulls = [grav[d, p] for d in range(3)]
         moms = [chip[core, d + 1, p] for d in range(3)]
         delta[0, p] = -balance[0]
@@ -261,9 +282,9 @@
         delta[4, p] = (moms[0] * pulls[0] + moms[1] * pulls[1] + moms[2] * pulls[2]) - balance[4]
         return after
 
-    face = face_x(1)
-    for p in range(8):
-        face = plane(p, face)
+    edge = face(0)
+    for p in range(8):
+        edge = plane(p, edge)
 
     start = plan[0]
     for f in range(5):
@@ -328,7 +349,8 @@
     rows = lax.all_to_all(packed, "x", 0, 0, tiled=True)
     chip = lax.all_gather(cs, "c")
     boxes, chip = lax.optimization_barrier((boxes, chip))
-    (plan,) = call(plan_kernel, [(3,)], "ss", [], ids, boxes)
+    plan, inner, third = call(
+        plan_kernel, [(3,), (5, 9, 8, 128), (5, 8, 8, 128)], "ssv", [pltpu.VMEM((5, 12, 8, 128), F32)], ids, boxes, chip)
     rows, plan = lax.optimization_barrier((rows, plan))
     rows = lax.all_gather(rows, "c")
     pair, red = call(pack_planes_kernel, [(56, 8, 128), (n_z, 8, 128)], "svv", [], ids, chip, rows)
@@ -342,9 +364,9 @@
     phi, delta, send = call(
         main_kernel,
         [(8, 8, 128), state, (10, 4, 8, 128)],
-        "ssvvvv",
+        "ssvvvvvv",
         [pltpu.VMEM(size, F32) for size in sizes],
-        ids, plan, loc, chip, rows, pairs)
+        ids, plan, loc, chip, rows, inner, third, pairs)
     delta, red = lax.optimization_barrier((delta, red))
     (red,) = call(fold_kernel, [(n_y, 128)], "v", [], red)
     red = lax.all_to_all(red.reshape(n_y, 1, 128), "y", 0, 0, tiled=True)

time: 64.3 us -> 63.9 us (level)
  no operation moved by 1% of the time
where the time goes in v5:
time: 63.9 us; the launch traced here: 63.4 us
  starting transfers between devices  36.5 us (57%)
  Pallas kernels  9.01 us (14%)
  blocking collectives  8.5 us (13%)
  waiting for transfers between devices  7.73 us (12%)
  local copies, waits for them, and re-layouts  0.92 us (1%)
  between operations  0.7 us (1%)
    all_to_all x1, starting transfers between devices, shards(): rows = lax.all_to_all(packed, 'x', 0, 0, tiled=True)  13.1 us
    ppermute x1, starting transfers between devices, shards(): pair = lax.ppermute(pair, BOX, mates)  9.16 us
    pallas_call x6, Pallas kernels, call(): pl.pallas_call(kernel, out_shape=shapes, in_specs=[pl.BlockSpec(memory_sp...  9.01 us
    ppermute x1, starting transfers between devices, shards(): came = lax.ppermute(send, BOX, mates)  7.24 us
    all_to_all x1, waiting for transfers between devices, shards(): red = lax.all_to_all(red.reshape(n_y, 1, 128), 'y', 0, 0, tiled=True)  5.57 us
    all_to_all x1, starting transfers between devices, shards(): red = lax.all_to_all(red.reshape(n_y, 1, 128), 'y', 0, 0, tiled=True)  3.51 us
    all_to_all x1, starting transfers between devices, shards(): red = lax.all_to_all(red, 'z', 0, 0, tiled=True)  3.51 us
    all_gather x1, blocking collectives, shards(): rows = lax.all_gather(rows, 'c')  2.19 us
  transfers between devices with their start and end apart: 5, of which 3 were waited for; matrix products, arithmetic and copies ran while one was open for 0% of the time, Pallas kernels for 8%

profile of v5, /device:TPU:2, one launch (start us, length us, event | category | flops | bytes accessed | tf_op | source)
XLA Modules:
  0.0 63.4 jit_solution(15942183576303581423)
XLA Ops:
  0.6 0.1 pad_add_fusion.ids
  0.7 0.0 copy-start
  0.7 0.9 %copy-done = f32[5,8,8,128]{3,2,1,0:T(8,128)S(1)} copy-done((f32[5,8,8,128]{3,2,1,0:T(8,128)S(1)}, f32[5,8,8,128]{3,2,1,0:T(8,128)}, u32[]{:S(2)}) %copy-start) | copy-done | bytes 163864
  1.6 1.4 %shard_map.41 = (f32[4,17,8,128]{3,2,1,0:T(8,128)}, f32[8,128]{1,0:T(8,128)S(1)}) custom-call(s32[2]{0:T(128)S(1)} %pad_add_fusion.ids, f32[5,8,8,128]{3,2,1,0:T(8,128)S(1)} %copy-done), custom_call_target="tpu_custom_call" | custom-call | tf_op jit(solution)/shard_map/pallas_call | solution.py:331
  3.1 0.0 copy-start.1
  3.1 13.1 %all-to-all-start = ((f32[4,17,8,128]{3,2,1,0:T(8,128)}), f32[4,17,8,128]{3,2,1,0:T(8,128)S(1)}, u32[]{:S(2)}, u32[]{:S(2)}) async-start(f32[4,17,8,128]{3,2,1,0:T(8,128)} %get-tuple-element.18), calls=%async_computation | async-start | bytes 557056 | tf_op jit(solution)/shard_map/all_to_all | solution.py:349
  16.2 0.0 copy-done.1
  16.2 0.0 copy-start.2
  16.2 2.2 %all-gather = f32[10,8,8,128]{3,2,1,0:T(8,128)S(1)} all-gather(f32[5,8,8,128]{3,2,1,0:T(8,128)S(1)} %copy-done.1), channel_id=2, replica_groups=mesh['y'=8,'z'=12,'c'=2,'x'=4] {'c'}, dimensions={0}, use_global_device_ids=true | all-gather | bytes 491520 | tf_op jit(solution)/shard_map/all_gather | solution.py:350
  18.3 0.0 copy-done.2
  18.3 1.5 %shard_map.42 = (s32[3]{0:T(128)S(1)}, f32[5,9,8,128]{3,2,1,0:T(8,128)S(1)}, f32[5,8,8,128]{3,2,1,0:T(8,128)S(1)}) custom-call(s32[2]{0:T(128)S(1)} %pad_add_fusion.ids, s32[384]{0:T(512)S(1)} %copy-done.2, f32[2,5,8,8,128]{4,3,2,1,0:T(8,128)S(1)} %bitcast.10), custom_call_target="tpu_custom_call" | custom-call | tf_op jit(solution)/shard_map/pallas_call | solution.py:331
  19.8 1.7 %all-to-all-done = f32[4,17,8,128]{3,2,1,0:T(8,128)S(1)} async-done(((f32[4,17,8,128]{3,2,1,0:T(8,128)}), f32[4,17,8,128]{3,2,1,0:T(8,128)S(1)}, u32[]{:S(2)}, u32[]{:S(2)}) %all-to-all-start) | async-done | bytes 278560 | tf_op jit(solution)/shard_map/all_to_all | solution.py:349
  21.5 2.2 %all-gather.1 = f32[8,17,8,128]{3,2,1,0:T(8,128)S(1)} all-gather(f32[4,17,8,128]{3,2,1,0:T(8,128)S(1)} %all-to-all-done), channel_id=3, replica_groups=mesh['y'=8,'z'=12,'c'=2,'x'=4] {'c'}, dimensions={0}, use_global_device_ids=true | all-gather | bytes 835584 | tf_op jit(solution)/shard_map/all_gather | solution.py:355
  23.7 1.2 %shard_map.43 = (f32[56,8,128]{2,1,0:T(8,128)S(1)}, f32[12,8,128]{2,1,0:T(8,128)}) custom-call(s32[2]{0:T(128)S(1)} %pad_add_fusion.ids, f32[2,5,8,8,128]{4,3,2,1,0:T(8,128)S(1)} %bitcast.11, f32[2,4,17,8,128]{4,3,2,1,0:T(8,128)S(1)} %bitcast.14), custom_call_target="tpu_custom_call" | custom-call | tf_op jit(solution)/shard_map/pallas_call | solution.py:331
  24.9 9.2 %collective-permute-start = (f32[56,8,128]{2,1,0:T(8,128)S(1)}, f32[56,8,128]{2,1,0:T(8,128)S(1)}, u32[]{:S(2)}, u32[]{:S(2)}) collective-permute-start(f32[56,8,128]{2,1,0:T(8,128)S(1)} %get-tuple-element.27), channel_id=1, source_target_pairs={{0,764},{4,8},{8,4},{12,16},{16,12},{20,24},{24,20},{28,32},{32,28... | collective-permute-start | bytes 688136 | tf_op jit(solution)/shard_map/ppermute | solution.py:357
  34.0 3.5 %all-to-all-start.1 = ((f32[12,8,128]{2,1,0:T(8,128)}), f32[12,8,128]{2,1,0:T(8,128)S(1)}, u32[]{:S(2)}, u32[]{:S(2)}) async-start(f32[12,8,128]{2,1,0:T(8,128)} %get-tuple-element.29), calls=%async_computation.1 | async-start | bytes 98304 | tf_op jit(solution)/shard_map/all_to_all | solution.py:358
  37.6 0.5 collective-permute-done
  38.0 2.1 %all-gather.2 = f32[112,8,128]{2,1,0:T(8,128)S(1)} all-gather(f32[56,8,128]{2,1,0:T(8,128)S(1)} %collective-permute-done), channel_id=4, replica_groups=mesh['y'=8,'z'=12,'c'=2,'x'=4] {'c'}, dimensions={0}, use_global_device_ids=true | all-gather | bytes 688128 | tf_op jit(solution)/shard_map/all_gather | solution.py:359
  40.1 3.0 %shard_map.44 = (f32[8,8,128]{2,1,0:T(8,128)S(1)}, f32[5,8,8,128]{3,2,1,0:T(8,128)S(1)}, f32[10,4,8,128]{3,2,1,0:T(8,128)S(1)}) custom-call(s32[2]{0:T(128)S(1)} %pad_add_fusion.ids, s32[3]{0:T(128)S(1)} %get-tuple-element.22.plan.refs_0_, f32[8,128]{1,0:T(8,128)S(1)} %get-tuple-element.23.loc.refs_1_, f32[2,5,8,8,128]{4,3,2,1,0:T(8,128)S(1)} %bitcast.12, ...), custom_call_target="tpu_custom_call" | custom-call | tf_op jit(solution)/shard_map/pallas_call | solution.py:331
  43.1 7.2 %collective-permute-start.1 = (f32[10,4,8,128]{3,2,1,0:T(8,128)S(1)}, f32[10,4,8,128]{3,2,1,0:T(8,128)S(1)}, u32[]{:S(2)}, u32[]{:S(2)}) collective-permute-start(f32[10,4,8,128]{3,2,1,0:T(8,128)S(1)} %get-tuple-element.33), channel_id=1, source_target_pairs={{0,764},{4,8},{8,4},{12,16},{16,12},{20,24},{24,20},{28,32},{32,28... | collective-permute-start | bytes 491528 | tf_op jit(solution)/shard_map/ppermute | solution.py:373
  50.4 0.0 all-to-all-done.1.got
  50.4 0.6 shard_map.45
  51.0 3.5 %all-to-all-start.2 = ((f32[8,1,128]{2,1,0:T(1,128)}), f32[8,1,128]{2,1,0:T(1,128)S(1)}, u32[]{:S(2)}, u32[]{:S(2)}) async-start(f32[8,1,128]{2,1,0:T(1,128)} %bitcast.6), calls=%async_computation.2 | async-start | bytes 8192 | tf_op jit(solution)/shard_map/all_to_all | solution.py:372
  54.5 2.0 %all-gather.3 = f32[10,8,8,128]{3,2,1,0:T(8,128)S(1)} all-gather(f32[5,8,8,128]{3,2,1,0:T(8,128)S(1)} %get-tuple-element.31), channel_id=5, replica_groups=mesh['y'=8,'z'=12,'c'=2,'x'=4] {'c'}, dimensions={0}, use_global_device_ids=true | all-gather | bytes 491520 | tf_op jit(solution)/shard_map/all_gather | solution.py:374
  56.5 5.6 %all-to-all-done.2 = f32[8,1,128]{2,1,0:T(1,128)S(1)} async-done(((f32[8,1,128]{2,1,0:T(1,128)}), f32[8,1,128]{2,1,0:T(1,128)S(1)}, u32[]{:S(2)}, u32[]{:S(2)}) %all-to-all-start.2) | async-done | bytes 4128 | tf_op jit(solution)/shard_map/all_to_all | solution.py:372
  62.1 0.0 collective-permute-done.1.refs_6_
  62.1 1.3 %shard_map.46 = (f32[5,8,8,128]{3,2,1,0:T(8,128)}, f32[8,8,128]{2,1,0:T(8,128)}) custom-call(s32[3]{0:T(128)S(1)} %get-tuple-element.22.plan.refs_0_, f32[8,128]{1,0:T(8,128)S(1)} %get-tuple-element.23.loc.refs_1_, f32[8,128]{1,0:T(8,128)S(1)} %bitcast.18, f32[2,5,8,8,128]{4,3,2,1,0:T(8,128)S(1)} %bitcast.13, f32[2,5,8,8,128]{4,3,2,1,0:T(8,128)S(1)} %bitcast.17, ...), custom_call_target="tpu_custom_call" | custom-call | tf_op jit(solution)/shard_map/pallas_call | solution.py:331
Async XLA Ops:
  0.7 0.9 %copy-start = (f32[5,8,8,128]{3,2,1,0:T(8,128)S(1)}, f32[5,8,8,128]{3,2,1,0:T(8,128)}, u32[]{:S(2)}) copy-start(f32[5,8,8,128]{3,2,1,0:T(8,128)} %cs.1) | copy-start | bytes 491524
  3.1 13.1 %copy-start.1 = (f32[5,8,8,128]{3,2,1,0:T(8,128)S(1)}, f32[5,8,8,128]{3,2,1,0:T(8,128)}, u32[]{:S(2)}) copy-start(f32[5,8,8,128]{3,2,1,0:T(8,128)} %cs.1) | copy-start | bytes 491524
  3.1 18.4 %all-to-all-start = ((f32[4,17,8,128]{3,2,1,0:T(8,128)}), f32[4,17,8,128]{3,2,1,0:T(8,128)S(1)}, u32[]{:S(2)}, u32[]{:S(2)}) async-start(f32[4,17,8,128]{3,2,1,0:T(8,128)} %get-tuple-element.18), calls=%async_computation | async-start | bytes 557056 | tf_op jit(solution)/shard_map/all_to_all | solution.py:349
  16.2 2.2 %copy-start.2 = (s32[384]{0:T(512)S(1)}, s32[384]{0:T(512)}, u32[]{:S(2)}) copy-start(s32[384]{0:T(512)} %boxes) | copy-start | bytes 4612
  24.9 13.2 %collective-permute-start = (f32[56,8,128]{2,1,0:T(8,128)S(1)}, f32[56,8,128]{2,1,0:T(8,128)S(1)}, u32[]{:S(2)}, u32[]{:S(2)}) collective-permute-start(f32[56,8,128]{2,1,0:T(8,128)S(1)} %get-tuple-element.27), channel_id=1, source_target_pairs={{0,764},{4,8},{8,4},{12,16},{16,12},{20,24},{24,20},{28,32},{32,28... | collective-permute-start | bytes 688136 | tf_op jit(solution)/shard_map/ppermute | solution.py:357
  34.0 16.3 %all-to-all-start.1 = ((f32[12,8,128]{2,1,0:T(8,128)}), f32[12,8,128]{2,1,0:T(8,128)S(1)}, u32[]{:S(2)}, u32[]{:S(2)}) async-start(f32[12,8,128]{2,1,0:T(8,128)} %get-tuple-element.29), calls=%async_computation.1 | async-start | bytes 98304 | tf_op jit(solution)/shard_map/all_to_all | solution.py:358
  43.1 19.0 %collective-permute-start.1 = (f32[10,4,8,128]{3,2,1,0:T(8,128)S(1)}, f32[10,4,8,128]{3,2,1,0:T(8,128)S(1)}, u32[]{:S(2)}, u32[]{:S(2)}) collective-permute-start(f32[10,4,8,128]{3,2,1,0:T(8,128)S(1)} %get-tuple-element.33), channel_id=1, source_target_pairs={{0,764},{4,8},{8,4},{12,16},{16,12},{20,24},{24,20},{28,32},{32,28... | collective-permute-start | bytes 491528 | tf_op jit(solution)/shard_map/ppermute | solution.py:373
  51.0 11.1 %all-to-all-start.2 = ((f32[8,1,128]{2,1,0:T(1,128)}), f32[8,1,128]{2,1,0:T(1,128)S(1)}, u32[]{:S(2)}, u32[]{:S(2)}) async-start(f32[8,1,128]{2,1,0:T(1,128)} %bitcast.6), calls=%async_computation.2 | async-start | bytes 8192 | tf_op jit(solution)/shard_map/all_to_all | solution.py:372
